TPU v7x, 128 devices: a whole 4x4x4 slice. The times are simulated.
128 devices in a mesh: seq: 16 (over y, x_lo, core), tp: 8 (over x_hi, z).
Axes of the slice: x: 4 (x_hi: 2, x_lo: 2; x = x_hi * 2 + x_lo), y: 4, z: 4, core: 2. Of those that a mesh axis runs over, the one named last changes fastest.
Arguments:
- queries: bfloat16 [2, 4096, 3072], P(None, 'seq', 'tp'), may hold values from -8 to 8
- keys: bfloat16 [2, 4096, 3072], P(None, 'seq', 'tp'), may hold values from -8 to 8
- values: bfloat16 [2, 4096, 3072], P(None, 'seq', 'tp'), may hold values from -6 to 6
- block_order: int32 [256], P('seq'), may hold values from 0 to 255, each once
- out_weight: bfloat16 [3072, 5120], P('tp'), may hold values from -0.109375 to 0.109375
- out_grad: bfloat16 [2, 4096, 5120], P(None, 'seq', 'tp'), may hold values from -6 to 6
Outputs:
- mixed: bfloat16 [2, 4096, 5120], P(None, 'seq', 'tp')
- query_grad: bfloat16 [2, 4096, 3072], P(None, 'seq', 'tp')
- key_grad: bfloat16 [2, 4096, 3072], P(None, 'seq', 'tp')
- value_grad: bfloat16 [2, 4096, 3072], P(None, 'seq', 'tp')
- weight_grad: float32 [3072, 5120], P('tp', 'seq')
Inputs may be any that keep to these rules, and one draw needn't show every extreme that they name: `block_order`: a permutation of the block positions.
All inputs are finite; a program needn't handle non-finite values.
Results may differ from a plain program's by a relative error of at most 0.029.
Values may be sent and summed in bfloat16 or wider, within the bound.
A program may use at most 128 MiB of HBM per device.

v0:
```python
import math

import jax
import jax.numpy as jnp
from jax import lax
from jax.sharding import PartitionSpec as P

HEAD_SIZE = 128
BLOCK = 16


masked_score = -1e30


def shifted(block, axis, distance):
    devices = range(lax.axis_size(axis))
    route = [((i - distance) % len(devices), i) for i in devices]
    return lax.ppermute(block, axis, route)


def local(queries, keys, values, block_order, out_weight, out_grad):
    seq_count = lax.axis_size("seq")
    seq_rank = lax.axis_index("seq")
    local_rows = queries.shape[1]
    inner_local = queries.shape[2]
    head_count = inner_local // HEAD_SIZE
    block_rows = local_rows // BLOCK
    scale_factor = 1.0 / math.sqrt(HEAD_SIZE)
    all_positions = lax.all_gather(block_order, "seq", axis=0, tiled=True)
    offsets = jnp.arange(local_rows, dtype=jnp.int32) % BLOCK
    own_position = jnp.repeat(block_order, BLOCK)
    query_position = jnp.concatenate([own_position, own_position])
    query_offset = jnp.concatenate([offsets, offsets])
    noisy_row = jnp.arange(2 * local_rows, dtype=jnp.int32) >= local_rows

    def visible(source):
        key_position = jnp.repeat(
            lax.dynamic_slice_in_dim(all_positions, source * block_rows, block_rows), BLOCK
        )
        earlier = key_position[None, :] < query_position[:, None]
        causal = earlier | (key_position[None, :] == query_position[:, None]) & (
            offsets[None, :] <= query_offset[:, None]
        )
        return jnp.where(noisy_row[:, None], earlier, causal)[None]

    query_heads = queries.reshape(2 * local_rows, head_count, HEAD_SIZE)
    noisy_queries = queries[1].reshape(block_rows, BLOCK, head_count, HEAD_SIZE)
    noisy_keys = keys[1].reshape(block_rows, BLOCK, head_count, HEAD_SIZE)
    noisy_values = values[1].reshape(block_rows, BLOCK, head_count, HEAD_SIZE)
    clean_keys = keys[0]
    clean_values = values[0]
    self_block_scores = (
        jnp.einsum("bqhd,bkhd->hbqk", noisy_queries, noisy_keys, preferred_element_type=jnp.float32)
        * scale_factor
    )
    own_top = jnp.max(self_block_scores, axis=3)
    self_exponent = jnp.exp(self_block_scores - own_top[..., None])
    own_total = jnp.sum(self_exponent, axis=3).reshape(head_count, local_rows)
    self_accumulator = jnp.einsum(
        "hbqk,bkhd->hbqd",
        self_exponent.astype(jnp.bfloat16),
        noisy_values,
        preferred_element_type=jnp.float32,
    ).reshape(head_count, local_rows, HEAD_SIZE)
    start_top = jnp.concatenate(
        [
            jnp.full((head_count, local_rows), masked_score, jnp.float32),
            own_top.reshape(head_count, local_rows),
        ],
        axis=1,
    )
    start_total = jnp.concatenate(
        [jnp.zeros((head_count, local_rows), jnp.float32), own_total], axis=1
    )
    start_acc = jnp.concatenate(
        [jnp.zeros((head_count, local_rows, HEAD_SIZE), jnp.float32), self_accumulator], axis=1
    )
    start_state = (start_top, start_total, start_acc)

    def forward_tile(carried, key_piece, value_piece, source):
        running_top, running_total, running_acc = carried
        allowed = visible(source)
        scores = (
            jnp.einsum(
                "qhd,khd->hqk",
                query_heads,
                key_piece.reshape(local_rows, head_count, HEAD_SIZE),
                preferred_element_type=jnp.float32,
            )
            * scale_factor
        )
        scores = jnp.where(allowed, scores, masked_score)
        new_top = jnp.maximum(running_top, jnp.max(scores, axis=2))
        weights = jnp.where(allowed, jnp.exp(scores - new_top[..., None]), 0.0)
        factor = jnp.exp(running_top - new_top)
        new_total = running_total * factor + jnp.sum(weights, axis=2)
        new_acc = running_acc * factor[..., None] + jnp.einsum(
            "hqk,khd->hqd",
            weights.astype(jnp.bfloat16),
            value_piece.reshape(local_rows, head_count, HEAD_SIZE),
            preferred_element_type=jnp.float32,
        )
        return (new_top, new_total, new_acc)

    def forward_turn(turn_index, carried):
        state_now, key_now, value_now = carried
        source = (seq_rank - turn_index) % seq_count
        state_now = forward_tile(state_now, key_now, value_now, source)
        key_now, value_now = shifted((key_now, value_now), "seq", 1)
        return (state_now, key_now, value_now)

    final_state, last_keys, last_values = lax.fori_loop(
        0, seq_count - 1, forward_turn, (start_state, clean_keys, clean_values)
    )
    final_state = forward_tile(final_state, last_keys, last_values, (seq_rank + 1) % seq_count)
    final_top, final_total, final_acc = final_state
    log_total = final_top + jnp.log(final_total)
    attention_heads = final_acc / final_total[..., None]
    attention = (
        jnp.transpose(attention_heads, (1, 0, 2))
        .reshape(2 * local_rows, inner_local)
        .astype(jnp.bfloat16)
    )
    partial_mix = jnp.dot(attention, out_weight, preferred_element_type=jnp.float32).reshape(
        2, local_rows, out_weight.shape[1]
    )
    mixed = lax.psum_scatter(
        partial_mix.astype(jnp.bfloat16), "tp", scatter_dimension=2, tiled=True
    )
    full_grad = lax.all_gather(out_grad, "tp", axis=2, tiled=True).reshape(
        2 * local_rows, out_weight.shape[1]
    )
    head_grad = jnp.einsum(
        "rd,cd->rc", full_grad, out_weight, preferred_element_type=jnp.float32
    ).astype(jnp.bfloat16)
    weight_term = jnp.einsum("rc,rd->cd", attention, full_grad, preferred_element_type=jnp.float32)
    weight_grad = lax.psum_scatter(
        weight_term.astype(jnp.bfloat16), "seq", scatter_dimension=1, tiled=True
    ).astype(jnp.float32)
    grad_heads = head_grad.reshape(2 * local_rows, head_count, HEAD_SIZE)
    row_delta = jnp.sum(
        grad_heads.astype(jnp.float32)
        * attention.reshape(2 * local_rows, head_count, HEAD_SIZE).astype(jnp.float32),
        axis=2,
    ).T

    def backward_tile(key_piece, value_piece, source):
        allowed = visible(source)
        key_heads = key_piece.reshape(local_rows, head_count, HEAD_SIZE)
        value_heads = value_piece.reshape(local_rows, head_count, HEAD_SIZE)
        scores = (
            jnp.einsum("qhd,khd->hqk", query_heads, key_heads, preferred_element_type=jnp.float32)
            * scale_factor
        )
        scores = jnp.where(allowed, scores, masked_score)
        prob_weights = jnp.where(allowed, jnp.exp(scores - log_total[..., None]), 0.0)
        value_term = jnp.einsum(
            "hqk,qhd->khd",
            prob_weights.astype(jnp.bfloat16),
            grad_heads,
            preferred_element_type=jnp.float32,
        )
        prob_grad = jnp.einsum(
            "qhd,khd->hqk", grad_heads, value_heads, preferred_element_type=jnp.float32
        )
        score_grad = (prob_weights * (prob_grad - row_delta[..., None])).astype(jnp.bfloat16)
        query_term = (
            jnp.einsum("hqk,khd->qhd", score_grad, key_heads, preferred_element_type=jnp.float32)
            * scale_factor
        )
        key_term = (
            jnp.einsum("hqk,qhd->khd", score_grad, query_heads, preferred_element_type=jnp.float32)
            * scale_factor
        )
        return (
            query_term,
            key_term.reshape(local_rows, inner_local),
            value_term.reshape(local_rows, inner_local),
        )

    zero_query = jnp.zeros((2 * local_rows, head_count, HEAD_SIZE), jnp.float32)
    zero_keys = jnp.zeros((local_rows, inner_local), jnp.float32)

    def pass_grads(key_sum, value_sum):
        return (
            shifted(key_sum.astype(jnp.bfloat16), "seq", 1).astype(key_sum.dtype),
            shifted(value_sum.astype(jnp.bfloat16), "seq", 1).astype(value_sum.dtype),
        )

    def backward_turn(turn_index, carried):
        query_sum, key_now, value_now, key_sum, value_sum = carried
        source = (seq_rank - turn_index) % seq_count
        query_term, key_term, value_term = backward_tile(key_now, value_now, source)
        key_sum, value_sum = pass_grads(key_sum + key_term, value_sum + value_term)
        key_now, value_now = shifted((key_now, value_now), "seq", 1)
        return (query_sum + query_term, key_now, value_now, key_sum, value_sum)

    query_sum, key_now, value_now, key_sum, value_sum = lax.fori_loop(
        0,
        seq_count - 1,
        backward_turn,
        (zero_query, clean_keys, clean_values, zero_keys, zero_keys),
    )
    query_term, key_term, value_term = backward_tile(key_now, value_now, (seq_rank + 1) % seq_count)
    query_sum = query_sum + query_term
    clean_key_grad, clean_value_grad = pass_grads(key_sum + key_term, value_sum + value_term)
    self_probabilities = jnp.exp(
        self_block_scores - log_total[:, local_rows:].reshape(head_count, block_rows, BLOCK, 1)
    )
    noisy_grads = grad_heads[local_rows:].reshape(block_rows, BLOCK, head_count, HEAD_SIZE)
    self_value_contribution = jnp.einsum(
        "hbqk,bqhd->bkhd",
        self_probabilities.astype(jnp.bfloat16),
        noisy_grads,
        preferred_element_type=jnp.float32,
    )
    self_probability_gradient = jnp.einsum(
        "bqhd,bkhd->hbqk", noisy_grads, noisy_values, preferred_element_type=jnp.float32
    )
    self_score_gradient = (
        self_probabilities
        * (
            self_probability_gradient
            - row_delta[:, local_rows:].reshape(head_count, block_rows, BLOCK, 1)
        )
    ).astype(jnp.bfloat16)
    self_query_contribution = (
        jnp.einsum(
            "hbqk,bkhd->bqhd", self_score_gradient, noisy_keys, preferred_element_type=jnp.float32
        )
        * scale_factor
    )
    self_key_contribution = (
        jnp.einsum(
            "hbqk,bqhd->bkhd",
            self_score_gradient,
            noisy_queries,
            preferred_element_type=jnp.float32,
        )
        * scale_factor
    )
    query_total = query_sum + jnp.concatenate(
        [
            jnp.zeros((local_rows, head_count, HEAD_SIZE), jnp.float32),
            self_query_contribution.reshape(local_rows, head_count, HEAD_SIZE),
        ],
        axis=0,
    )
    query_grad = query_total.reshape(2, local_rows, inner_local).astype(jnp.bfloat16)
    key_grad = jnp.stack(
        [clean_key_grad, self_key_contribution.reshape(local_rows, inner_local)]
    ).astype(jnp.bfloat16)
    value_grad = jnp.stack(
        [clean_value_grad, self_value_contribution.reshape(local_rows, inner_local)]
    ).astype(jnp.bfloat16)
    return (mixed, query_grad, key_grad, value_grad, weight_grad)


def solution(mesh):
    return jax.shard_map(
        local,
        mesh=mesh,
        in_specs=(
            P(None, "seq", "tp"),
            P(None, "seq", "tp"),
            P(None, "seq", "tp"),
            P("seq"),
            P("tp", None),
            P(None, "seq", "tp"),
        ),
        out_specs=(
            P(None, "seq", "tp"),
            P(None, "seq", "tp"),
            P(None, "seq", "tp"),
            P(None, "seq", "tp"),
            P("tp", "seq"),
        ),
        check_vma=False,
    )
```

profile of v0, /device:TPU:1, one launch (start us, length us, event | category | flops | bytes accessed | tf_op | source)
XLA Modules:
  0.0 547.5 jit_solution(11868428563665136756)
XLA Ops:
  11.1 11.5 %all-reduce.4 = s32[256]{0:T(256)} all-reduce(s32[256]{0:T(256)S(1)} %dynamic-update-slice), channel_id=1, replica_groups=mesh['seq'=16,'tp'=8] {'seq'}, use_global_device_ids=true, to_apply=%add.4 | all-reduce | flops 256 | bytes 2048
  29.1 152.9 %while.48 = (s32[]{:T(128)}, f32[3,512]{1,0:T(4,128)S(1)}, f32[3,512]{1,0:T(4,128)S(1)}, f32[3,512,128]{2,1,0:T(8,128)S(1)}, bf16[256,384]{0,1:T(8,128)(2,1)S(1)...) while((s32[]{:T(128)}, f32[3,512]{1,0:T(4,128)S(1)}, ...), condition=%wide.region_5.6_spmd.clone, body=%wide.region_2.5_spmd.clone.sunk | while | flops 206050320 | bytes 10071632 | solution.py:112
  61.9 7.5 %collective-permute-done = bf16[256,384]{0,1:T(8,128)(2,1)S(1)} collective-permute-done((bf16[256,384]{0,1:T(8,128)(2,1)S(1)}, bf16[256,384]{0,1:T(8,128)(2,1)S(1)}, u32[]{:S(2)}, u32[]{:S(2)}) %collective-permute-start) | collective-permute-done | bytes 196640 | tf_op jit(solution)/shard_map/while/body/eval_jaxpr/ppermute | solution.py:18
  78.5 8.7 %collective-permute-done = bf16[256,384]{0,1:T(8,128)(2,1)S(1)} collective-permute-done((bf16[256,384]{0,1:T(8,128)(2,1)S(1)}, bf16[256,384]{0,1:T(8,128)(2,1)S(1)}, u32[]{:S(2)}, u32[]{:S(2)}) %collective-permute-start) | collective-permute-done | bytes 196640 | tf_op jit(solution)/shard_map/while/body/eval_jaxpr/ppermute | solution.py:18
  110.5 5.4 collective-permute-done
  119.2 6.1 %collective-permute-done = bf16[256,384]{0,1:T(8,128)(2,1)S(1)} collective-permute-done((bf16[256,384]{0,1:T(8,128)(2,1)S(1)}, bf16[256,384]{0,1:T(8,128)(2,1)S(1)}, u32[]{:S(2)}, u32[]{:S(2)}) %collective-permute-start) | collective-permute-done | bytes 196640 | tf_op jit(solution)/shard_map/while/body/eval_jaxpr/ppermute | solution.py:18
  128.6 6.1 %collective-permute-done = bf16[256,384]{0,1:T(8,128)(2,1)S(1)} collective-permute-done((bf16[256,384]{0,1:T(8,128)(2,1)S(1)}, bf16[256,384]{0,1:T(8,128)(2,1)S(1)}, u32[]{:S(2)}, u32[]{:S(2)}) %collective-permute-start) | collective-permute-done | bytes 196640 | tf_op jit(solution)/shard_map/while/body/eval_jaxpr/ppermute | solution.py:18
  138.0 6.1 %collective-permute-done = bf16[256,384]{0,1:T(8,128)(2,1)S(1)} collective-permute-done((bf16[256,384]{0,1:T(8,128)(2,1)S(1)}, bf16[256,384]{0,1:T(8,128)(2,1)S(1)}, u32[]{:S(2)}, u32[]{:S(2)}) %collective-permute-start) | collective-permute-done | bytes 196640 | tf_op jit(solution)/shard_map/while/body/eval_jaxpr/ppermute | solution.py:18
  147.4 6.1 %collective-permute-done = bf16[256,384]{0,1:T(8,128)(2,1)S(1)} collective-permute-done((bf16[256,384]{0,1:T(8,128)(2,1)S(1)}, bf16[256,384]{0,1:T(8,128)(2,1)S(1)}, u32[]{:S(2)}, u32[]{:S(2)}) %collective-permute-start) | collective-permute-done | bytes 196640 | tf_op jit(solution)/shard_map/while/body/eval_jaxpr/ppermute | solution.py:18
  156.8 6.1 %collective-permute-done = bf16[256,384]{0,1:T(8,128)(2,1)S(1)} collective-permute-done((bf16[256,384]{0,1:T(8,128)(2,1)S(1)}, bf16[256,384]{0,1:T(8,128)(2,1)S(1)}, u32[]{:S(2)}, u32[]{:S(2)}) %collective-permute-start) | collective-permute-done | bytes 196640 | tf_op jit(solution)/shard_map/while/body/eval_jaxpr/ppermute | solution.py:18
  166.2 6.1 %collective-permute-done = bf16[256,384]{0,1:T(8,128)(2,1)S(1)} collective-permute-done((bf16[256,384]{0,1:T(8,128)(2,1)S(1)}, bf16[256,384]{0,1:T(8,128)(2,1)S(1)}, u32[]{:S(2)}, u32[]{:S(2)}) %collective-permute-start) | collective-permute-done | bytes 196640 | tf_op jit(solution)/shard_map/while/body/eval_jaxpr/ppermute | solution.py:18
  175.6 6.1 %collective-permute-done = bf16[256,384]{0,1:T(8,128)(2,1)S(1)} collective-permute-done((bf16[256,384]{0,1:T(8,128)(2,1)S(1)}, bf16[256,384]{0,1:T(8,128)(2,1)S(1)}, u32[]{:S(2)}, u32[]{:S(2)}) %collective-permute-start) | collective-permute-done | bytes 196640 | tf_op jit(solution)/shard_map/while/body/eval_jaxpr/ppermute | solution.py:18
  185.2 6.0 %convolution_convert_fusion.2 = bf16[512,384]{0,1:T(8,128)(2,1)S(1)} fusion(bf16[512,5120]{1,0:T(8,128)(2,1)} %bitcast.169, bf16[384,5120]{1,0:T(8,128)(2,1)} %param.14), kind=kOutput, calls=%fused_computation.53 | convolution fusion | flops 2013462528 | bytes 9568256 | tf_op jit(solution)/shard_map/rd,cd->rc/dot_general | solution.py:133
  201.4 6.7 %convolution_convert_fusion = bf16[2,256,5120]{2,1,0:T(8,128)(2,1)} fusion(bf16[384,5120]{1,0:T(8,128)(2,1)} %param.14, bf16[2,256,384]{1,0,2:T(2,128)(2,1)S(1)} %convert_element_type.141), kind=kOutput, calls=%fused_computation.33 | convolution fusion | flops 2015887360 | bytes 9568256 | tf_op jit(solution)/shard_map/dot_general | solution.py:124
  208.2 13.7 %copy.173 = bf16[2,256,5120]{1,0,2:T(2,128)(2,1)} copy(bf16[2,256,5120]{2,1,0:T(8,128)(2,1)} %convolution_convert_fusion) | data formatting | bytes 10485760
  221.8 5.8 %copy.177 = bf16[640,8,2,256]{3,1,2,0:T(8,128)(2,1)} copy(bf16[640,8,2,256]{3,2,1,0:T(2,128)(2,1)} %bitcast.150) | data formatting | bytes 10485760
  228.3 283.0 %while.49 = (s32[]{:T(128)}, f32[512,3,128]{2,0,1:T(8,128)S(1)}, bf16[256,384]{0,1:T(8,128)(2,1)}, bf16[256,384]{0,1:T(8,128)(2,1)}, f32[256,384]{0,1:T(8,128)S(...) while((s32[]{:T(128)}, f32[512,3,128]{2,0,1:T(8,128)S(1)}, ...), condition=%wide.region_11.12_spmd.clone, body=%wide.region_10.11_spmd.clone.sunk | while | flops 508725248 | bytes 18964164 | solution.py:198
  235.7 11.6 %collective-permute-done.5 = bf16[256,384]{0,1:T(8,128)(2,1)} collective-permute-done((bf16[256,384]{0,1:T(8,128)(2,1)}, bf16[256,384]{0,1:T(8,128)(2,1)}, u32[]{:S(2)}, u32[]{:S(2)}) %collective-permute-start.5) | collective-permute-done | bytes 196640 | tf_op jit(solution)/shard_map/while/body/eval_jaxpr/ppermute | solution.py:18
  248.2 4.7 collective-permute-done.4
  263.8 10.2 %collective-permute-done.5 = bf16[256,384]{0,1:T(8,128)(2,1)} collective-permute-done((bf16[256,384]{0,1:T(8,128)(2,1)}, bf16[256,384]{0,1:T(8,128)(2,1)}, u32[]{:S(2)}, u32[]{:S(2)}) %collective-permute-start.5) | collective-permute-done | bytes 196640 | tf_op jit(solution)/shard_map/while/body/eval_jaxpr/ppermute | solution.py:18
  301.5 13.3 %collective-permute-done.5 = bf16[256,384]{0,1:T(8,128)(2,1)} collective-permute-done((bf16[256,384]{0,1:T(8,128)(2,1)}, bf16[256,384]{0,1:T(8,128)(2,1)}, u32[]{:S(2)}, u32[]{:S(2)}) %collective-permute-start.5) | collective-permute-done | bytes 196640 | tf_op jit(solution)/shard_map/while/body/eval_jaxpr/ppermute | solution.py:18
  324.6 12.8 %collective-permute-done.5 = bf16[256,384]{0,1:T(8,128)(2,1)} collective-permute-done((bf16[256,384]{0,1:T(8,128)(2,1)}, bf16[256,384]{0,1:T(8,128)(2,1)}, u32[]{:S(2)}, u32[]{:S(2)}) %collective-permute-start.5) | collective-permute-done | bytes 196640 | tf_op jit(solution)/shard_map/while/body/eval_jaxpr/ppermute | solution.py:18
  347.1 13.0 %collective-permute-done.5 = bf16[256,384]{0,1:T(8,128)(2,1)} collective-permute-done((bf16[256,384]{0,1:T(8,128)(2,1)}, bf16[256,384]{0,1:T(8,128)(2,1)}, u32[]{:S(2)}, u32[]{:S(2)}) %collective-permute-start.5) | collective-permute-done | bytes 196640 | tf_op jit(solution)/shard_map/while/body/eval_jaxpr/ppermute | solution.py:18
  370.0 7.6 %collective-permute-done.5 = bf16[256,384]{0,1:T(8,128)(2,1)} collective-permute-done((bf16[256,384]{0,1:T(8,128)(2,1)}, bf16[256,384]{0,1:T(8,128)(2,1)}, u32[]{:S(2)}, u32[]{:S(2)}) %collective-permute-start.5) | collective-permute-done | bytes 196640 | tf_op jit(solution)/shard_map/while/body/eval_jaxpr/ppermute | solution.py:18
  (776 shorter events, 348.3 us)
Async XLA Ops:
  7.2 178.0 %all-gather.2.cloned.1.call-start = ((), (), s32[]{:S(2)}) async-start(), calls=%async_computation.2 | async-start | bytes 5898240 | tf_op jit(solution)/shard_map/all_gather | solution.py:130
  7.9 527.3 %reduce-scatter.5.cloned.1.call-start = ((), (), s32[]{:S(2)}) async-start(), calls=%async_computation.3 | async-start | bytes 4177920 | tf_op jit(solution)/shard_map/reduce_scatter | solution.py:137
  70.3 17.0 %collective-permute-start = (bf16[256,384]{0,1:T(8,128)(2,1)S(1)}, bf16[256,384]{0,1:T(8,128)(2,1)S(1)}, u32[]{:S(2)}, u32[]{:S(2)}) collective-permute-start(bf16[256,384]{0,1:T(8,128)(2,1)S(1)} %copy.219), channel_id=1, source_target_pairs={{120,0},{0,8},{8,16},{16,24},{24,32},{32,40},{40,48},{48,56},{56,6... | collective-permute-start | bytes 589832 | tf_op jit(solution)/shard_map/while/body/eval_jaxpr/ppermute | solution.py:18
  198.2 338.9 %reduce-scatter.7.cloned.1.call-start = ((), (), s32[]{:S(2)}) async-start(), calls=%async_computation.4 | async-start | bytes 5898240
  229.2 24.7 %collective-permute-start.2 = (bf16[256,384]{0,1:T(8,128)(2,1)S(1)}, bf16[256,384]{0,1:T(8,128)(2,1)}, u32[]{:S(2)}, u32[]{:S(2)}) collective-permute-start(bf16[256,384]{0,1:T(8,128)(2,1)S(1)} %copy.235), channel_id=1, source_target_pairs={{120,0},{0,8},{8,16},{16,24},{24,32},{32,40},{40,48},{48,56},{56,6... | collective-permute-start | bytes 589832 | tf_op jit(solution)/shard_map/while/body/eval_jaxpr/ppermute | solution.py:18
  230.2 23.8 %collective-permute-start.3 = (bf16[256,384]{0,1:T(8,128)(2,1)S(1)}, bf16[256,384]{0,1:T(8,128)(2,1)}, u32[]{:S(2)}, u32[]{:S(2)}) collective-permute-start(bf16[256,384]{0,1:T(8,128)(2,1)S(1)} %copy.236), channel_id=1, source_target_pairs={{120,0},{0,8},{8,16},{16,24},{24,32},{32,40},{40,48},{48,56},{56,6... | collective-permute-start | bytes 589832 | tf_op jit(solution)/shard_map/while/body/eval_jaxpr/ppermute | solution.py:18
  235.2 17.8 %collective-permute-start.4 = (bf16[256,384]{0,1:T(8,128)(2,1)}, bf16[256,384]{0,1:T(8,128)(2,1)}, u32[]{:S(2)}, u32[]{:S(2)}) collective-permute-start(bf16[256,384]{0,1:T(8,128)(2,1)} %fusion.136), channel_id=1, source_target_pairs={{120,0},{0,8},{8,16},{16,24},{24,32},{32,40},{40,48},{48,56},{56,6... | collective-permute-start | bytes 589832 | tf_op jit(solution)/shard_map/while/body/eval_jaxpr/ppermute | solution.py:18
  254.9 22.8 %collective-permute-start.2 = (bf16[256,384]{0,1:T(8,128)(2,1)S(1)}, bf16[256,384]{0,1:T(8,128)(2,1)}, u32[]{:S(2)}, u32[]{:S(2)}) collective-permute-start(bf16[256,384]{0,1:T(8,128)(2,1)S(1)} %copy.235), channel_id=1, source_target_pairs={{120,0},{0,8},{8,16},{16,24},{24,32},{32,40},{40,48},{48,56},{56,6... | collective-permute-start | bytes 589832 | tf_op jit(solution)/shard_map/while/body/eval_jaxpr/ppermute | solution.py:18
  258.3 19.4 %collective-permute-start.3 = (bf16[256,384]{0,1:T(8,128)(2,1)S(1)}, bf16[256,384]{0,1:T(8,128)(2,1)}, u32[]{:S(2)}, u32[]{:S(2)}) collective-permute-start(bf16[256,384]{0,1:T(8,128)(2,1)S(1)} %copy.236), channel_id=1, source_target_pairs={{120,0},{0,8},{8,16},{16,24},{24,32},{32,40},{40,48},{48,56},{56,6... | collective-permute-start | bytes 589832 | tf_op jit(solution)/shard_map/while/body/eval_jaxpr/ppermute | solution.py:18
  278.6 15.5 %collective-permute-start.2 = (bf16[256,384]{0,1:T(8,128)(2,1)S(1)}, bf16[256,384]{0,1:T(8,128)(2,1)}, u32[]{:S(2)}, u32[]{:S(2)}) collective-permute-start(bf16[256,384]{0,1:T(8,128)(2,1)S(1)} %copy.235), channel_id=1, source_target_pairs={{120,0},{0,8},{8,16},{16,24},{24,32},{32,40},{40,48},{48,56},{56,6... | collective-permute-start | bytes 589832 | tf_op jit(solution)/shard_map/while/body/eval_jaxpr/ppermute | solution.py:18
  295.1 22.1 %collective-permute-start.2 = (bf16[256,384]{0,1:T(8,128)(2,1)S(1)}, bf16[256,384]{0,1:T(8,128)(2,1)}, u32[]{:S(2)}, u32[]{:S(2)}) collective-permute-start(bf16[256,384]{0,1:T(8,128)(2,1)S(1)} %copy.235), channel_id=1, source_target_pairs={{120,0},{0,8},{8,16},{16,24},{24,32},{32,40},{40,48},{48,56},{56,6... | collective-permute-start | bytes 589832 | tf_op jit(solution)/shard_map/while/body/eval_jaxpr/ppermute | solution.py:18
  296.0 21.2 %collective-permute-start.3 = (bf16[256,384]{0,1:T(8,128)(2,1)S(1)}, bf16[256,384]{0,1:T(8,128)(2,1)}, u32[]{:S(2)}, u32[]{:S(2)}) collective-permute-start(bf16[256,384]{0,1:T(8,128)(2,1)S(1)} %copy.236), channel_id=1, source_target_pairs={{120,0},{0,8},{8,16},{16,24},{24,32},{32,40},{40,48},{48,56},{56,6... | collective-permute-start | bytes 589832 | tf_op jit(solution)/shard_map/while/body/eval_jaxpr/ppermute | solution.py:18
  299.6 15.2 %collective-permute-start.5 = (bf16[256,384]{0,1:T(8,128)(2,1)}, bf16[256,384]{0,1:T(8,128)(2,1)}, u32[]{:S(2)}, u32[]{:S(2)}) collective-permute-start(bf16[256,384]{0,1:T(8,128)(2,1)} %fusion.138), channel_id=1, source_target_pairs={{120,0},{0,8},{8,16},{16,24},{24,32},{32,40},{40,48},{48,56},{56,6... | collective-permute-start | bytes 589832 | tf_op jit(solution)/shard_map/while/body/eval_jaxpr/ppermute | solution.py:18
  301.1 15.2 %collective-permute-start.4 = (bf16[256,384]{0,1:T(8,128)(2,1)}, bf16[256,384]{0,1:T(8,128)(2,1)}, u32[]{:S(2)}, u32[]{:S(2)}) collective-permute-start(bf16[256,384]{0,1:T(8,128)(2,1)} %fusion.136), channel_id=1, source_target_pairs={{120,0},{0,8},{8,16},{16,24},{24,32},{32,40},{40,48},{48,56},{56,6... | collective-permute-start | bytes 589832 | tf_op jit(solution)/shard_map/while/body/eval_jaxpr/ppermute | solution.py:18
  318.2 21.6 %collective-permute-start.2 = (bf16[256,384]{0,1:T(8,128)(2,1)S(1)}, bf16[256,384]{0,1:T(8,128)(2,1)}, u32[]{:S(2)}, u32[]{:S(2)}) collective-permute-start(bf16[256,384]{0,1:T(8,128)(2,1)S(1)} %copy.235), channel_id=1, source_target_pairs={{120,0},{0,8},{8,16},{16,24},{24,32},{32,40},{40,48},{48,56},{56,6... | collective-permute-start | bytes 589832 | tf_op jit(solution)/shard_map/while/body/eval_jaxpr/ppermute | solution.py:18
  319.1 20.7 %collective-permute-start.3 = (bf16[256,384]{0,1:T(8,128)(2,1)S(1)}, bf16[256,384]{0,1:T(8,128)(2,1)}, u32[]{:S(2)}, u32[]{:S(2)}) collective-permute-start(bf16[256,384]{0,1:T(8,128)(2,1)S(1)} %copy.236), channel_id=1, source_target_pairs={{120,0},{0,8},{8,16},{16,24},{24,32},{32,40},{40,48},{48,56},{56,6... | collective-permute-start | bytes 589832 | tf_op jit(solution)/shard_map/while/body/eval_jaxpr/ppermute | solution.py:18
  340.7 21.9 %collective-permute-start.2 = (bf16[256,384]{0,1:T(8,128)(2,1)S(1)}, bf16[256,384]{0,1:T(8,128)(2,1)}, u32[]{:S(2)}, u32[]{:S(2)}) collective-permute-start(bf16[256,384]{0,1:T(8,128)(2,1)S(1)} %copy.235), channel_id=1, source_target_pairs={{120,0},{0,8},{8,16},{16,24},{24,32},{32,40},{40,48},{48,56},{56,6... | collective-permute-start | bytes 589832 | tf_op jit(solution)/shard_map/while/body/eval_jaxpr/ppermute | solution.py:18
  341.7 20.9 %collective-permute-start.3 = (bf16[256,384]{0,1:T(8,128)(2,1)S(1)}, bf16[256,384]{0,1:T(8,128)(2,1)}, u32[]{:S(2)}, u32[]{:S(2)}) collective-permute-start(bf16[256,384]{0,1:T(8,128)(2,1)S(1)} %copy.236), channel_id=1, source_target_pairs={{120,0},{0,8},{8,16},{16,24},{24,32},{32,40},{40,48},{48,56},{56,6... | collective-permute-start | bytes 589832 | tf_op jit(solution)/shard_map/while/body/eval_jaxpr/ppermute | solution.py:18
  363.6 17.0 %collective-permute-start.2 = (bf16[256,384]{0,1:T(8,128)(2,1)S(1)}, bf16[256,384]{0,1:T(8,128)(2,1)}, u32[]{:S(2)}, u32[]{:S(2)}) collective-permute-start(bf16[256,384]{0,1:T(8,128)(2,1)S(1)} %copy.235), channel_id=1, source_target_pairs={{120,0},{0,8},{8,16},{16,24},{24,32},{32,40},{40,48},{48,56},{56,6... | collective-permute-start | bytes 589832 | tf_op jit(solution)/shard_map/while/body/eval_jaxpr/ppermute | solution.py:18
  364.5 16.1 %collective-permute-start.3 = (bf16[256,384]{0,1:T(8,128)(2,1)S(1)}, bf16[256,384]{0,1:T(8,128)(2,1)}, u32[]{:S(2)}, u32[]{:S(2)}) collective-permute-start(bf16[256,384]{0,1:T(8,128)(2,1)S(1)} %copy.236), channel_id=1, source_target_pairs={{120,0},{0,8},{8,16},{16,24},{24,32},{32,40},{40,48},{48,56},{56,6... | collective-permute-start | bytes 589832 | tf_op jit(solution)/shard_map/while/body/eval_jaxpr/ppermute | solution.py:18
  412.9 16.8 %collective-permute-start.2 = (bf16[256,384]{0,1:T(8,128)(2,1)S(1)}, bf16[256,384]{0,1:T(8,128)(2,1)}, u32[]{:S(2)}, u32[]{:S(2)}) collective-permute-start(bf16[256,384]{0,1:T(8,128)(2,1)S(1)} %copy.235), channel_id=1, source_target_pairs={{120,0},{0,8},{8,16},{16,24},{24,32},{32,40},{40,48},{48,56},{56,6... | collective-permute-start | bytes 589832 | tf_op jit(solution)/shard_map/while/body/eval_jaxpr/ppermute | solution.py:18
  430.7 15.4 %collective-permute-start.2 = (bf16[256,384]{0,1:T(8,128)(2,1)S(1)}, bf16[256,384]{0,1:T(8,128)(2,1)}, u32[]{:S(2)}, u32[]{:S(2)}) collective-permute-start(bf16[256,384]{0,1:T(8,128)(2,1)S(1)} %copy.235), channel_id=1, source_target_pairs={{120,0},{0,8},{8,16},{16,24},{24,32},{32,40},{40,48},{48,56},{56,6... | collective-permute-start | bytes 589832 | tf_op jit(solution)/shard_map/while/body/eval_jaxpr/ppermute | solution.py:18
  447.0 15.4 %collective-permute-start.2 = (bf16[256,384]{0,1:T(8,128)(2,1)S(1)}, bf16[256,384]{0,1:T(8,128)(2,1)}, u32[]{:S(2)}, u32[]{:S(2)}) collective-permute-start(bf16[256,384]{0,1:T(8,128)(2,1)S(1)} %copy.235), channel_id=1, source_target_pairs={{120,0},{0,8},{8,16},{16,24},{24,32},{32,40},{40,48},{48,56},{56,6... | collective-permute-start | bytes 589832 | tf_op jit(solution)/shard_map/while/body/eval_jaxpr/ppermute | solution.py:18
  479.0 16.3 %collective-permute-start.2 = (bf16[256,384]{0,1:T(8,128)(2,1)S(1)}, bf16[256,384]{0,1:T(8,128)(2,1)}, u32[]{:S(2)}, u32[]{:S(2)}) collective-permute-start(bf16[256,384]{0,1:T(8,128)(2,1)S(1)} %copy.235), channel_id=1, source_target_pairs={{120,0},{0,8},{8,16},{16,24},{24,32},{32,40},{40,48},{48,56},{56,6... | collective-permute-start | bytes 589832 | tf_op jit(solution)/shard_map/while/body/eval_jaxpr/ppermute | solution.py:18
  (98 other events, 756.1 us)
Sparse Core Ops, SparseCore 0:
  10.4 93.7 all-gather.1
  198.3 77.8 reduce-scatter.4
  280.5 108.3 reduce-scatter.6
where the time goes:
time: 557 us; the launch traced here: 548 us
  waiting for transfers between devices  185 us (33%)
  local copies, waits for them, and re-layouts  101 us (18%)
  matrix products  88.8 us (16%)
  starting transfers between devices  73.5 us (13%)
  other arithmetic  69.4 us (12%)
  between operations  15.1 us (3%)
  blocking collectives  11.5 us (2%)
    ppermute x92, waiting for transfers between devices, shifted(): return lax.ppermute(block, axis, route)  184 us
    ppermute x92, starting transfers between devices, shifted(): return lax.ppermute(block, axis, route)  73.2 us
    unnamed x67, local copies, waits for them, and re-layouts  35.2 us
    while x75, local copies, waits for them, and re-layouts  28.3 us
    dot_general x16, matrix products, backward_tile(): jnp.einsum('qhd,khd->hqk', query_heads, key_heads, preferred_element_type...  22.4 us
    dynamic_slice x31, local copies, waits for them, and re-layouts, visible(): lax.dynamic_slice_in_dim(all_positions, source * block_rows, block_rows)  21.2 us
    convert_element_type x15, other arithmetic, pass_grads(): shifted(value_sum.astype(jnp.bfloat16), 'seq', 1).astype(value_sum.dtype)  14.3 us
    convert_element_type x15, other arithmetic, pass_grads(): shifted(key_sum.astype(jnp.bfloat16), 'seq', 1).astype(key_sum.dtype)  14.3 us
  transfers between devices with their start and end apart: 95, of which 58 were waited for; matrix products, arithmetic and copies ran while one was open for 44% of the time, Pallas kernels for 0%

commit v1 on v0

v1 whole, which is shorter than its diff:
```python
import functools
import math

import jax
import jax.numpy as jnp
from jax import lax
from jax.experimental import pallas as pl
from jax.experimental.pallas import tpu as pltpu
from jax.sharding import PartitionSpec as P

HEAD_SIZE = 128
BLOCK = 16
HEADS_DEV = 3
ROWS = 256
BOTH = 2 * ROWS
POS_ROWS = ROWS // BLOCK
INNER_DEV = HEADS_DEV * HEAD_SIZE
WIDTH = 640
MESH = pl.DeviceIdType.MESH
F32 = jnp.float32
BF16 = jnp.bfloat16
MASKED = -1e30
LOWEST = -1e29
LOG2_SCALE = math.log2(math.e) / math.sqrt(HEAD_SIZE)
SCALE = 1.0 / math.sqrt(HEAD_SIZE)


def dot(a, b):
    return lax.dot_general(a, b, (((1,), (0,)), ((), ())), preferred_element_type=F32)


def dot_nt(a, b):
    return lax.dot_general(a, b, (((1,), (1,)), ((), ())), preferred_element_type=F32)


def dot_tn(a, b):
    return lax.dot_general(a, b, (((0,), (0,)), ((), ())), preferred_element_type=F32)


def remote(src, dst, send_sem, recv_sem, device):
    return pltpu.make_async_remote_copy(
        src_ref=src,
        dst_ref=dst,
        send_sem=send_sem,
        recv_sem=recv_sem,
        device_id=device,
        device_id_type=MESH,
    )


class RingReduce:
    def __init__(self, piece, via, ring, cross, send, recv, plus, minus, partner):
        self.piece, self.via, self.ring, self.cross = piece, via, ring, cross
        self.send, self.recv = send, recv
        self.plus, self.minus, self.partner = plus, minus, partner

    def copy(self, kind, p, n):
        if kind == "cross":
            return remote(
                self.piece(1, 0), self.cross, self.send.at[12], self.recv.at[12], self.partner
            )
        at = 6 * p + 2 * ("far", "near", "joint").index(kind) + n
        half = 1 - n if kind == "near" else n
        source = self.piece(p, 2 if kind == "far" else (1, 3)[n]).at[half]
        target = self.via.at[p, n] if kind == "far" else self.ring.at[p, n, half]
        device = (self.plus, self.minus)[n]
        return remote(source, target, self.send.at[at], self.recv.at[at], device)

    def start(self, kind, p, which=(0, 1)):
        for n in which:
            self.copy(kind, p, n).start()

    def join(self, p, which=(0, 1)):
        for n in which:
            self.copy("far", p, n).wait_recv()
            target = self.piece(p, (1, 3)[n])
            target[n] = (target[n].astype(F32) + self.via[p, n].astype(F32)).astype(BF16)
            self.copy("joint", p, n).start()

    def gathered(self, p):
        for kind in ("near", "joint"):
            for n in (0, 1):
                self.copy(kind, p, n).wait_recv()
        own = self.piece(p, 0)
        return own[...].astype(F32) + self.ring[p, 0].astype(F32) + self.ring[p, 1].astype(F32)

    def to_partner(self):
        total = self.gathered(1)
        self.piece(1, 0)[...] = total.astype(BF16)
        self.copy("cross", 1, 0).start()

    def result(self):
        total = self.gathered(0)
        self.copy("cross", 1, 0).wait_recv()
        return total + self.cross[...].astype(F32)

    def finish(self):
        for p in (0, 1):
            for kind in ("far", "near", "joint"):
                for n in (0, 1):
                    self.copy(kind, p, n).wait_send()
        self.copy("cross", 1, 0).wait_send()


def layer_kernel(
    q_ref, own_kv, noisy_kv, w_ref, og_ref, limit_ref,
    mixed_ref, qg_ref, kg_ref, vg_ref, wg_ref,
    kv, og, qt, acc, stat, att_t, att, bias, head_t, head, dq,
    mixp, m_via, m_ring, m_cross,
    w_pair, w_out, w_recv, w_via, w_ring, w_cross, w_final, w_other,
    t_out, t_recv, t_mine, t_via, t_ring, t_cross,
    kv_send, kv_recv, og_send, og_recv,
    m_send, m_rsem, w_send, w_rsem, ws_send, ws_recv, wf_sem,
    t_send, t_rsem, ts_send, ts_recv,
):
    s = lax.axis_index("seq")
    t = lax.axis_index("tp")
    y, x, c = s // 4, (s // 2) % 2, s % 2
    xh, z = t // 4, t % 4

    def slot(ys, xs, cs):
        return (ys * 2 + xs) * 2 + cs

    y_plus = {"seq": slot((y + 1) % 4, x, c)}
    y_minus = {"seq": slot((y + 3) % 4, x, c)}
    x_near = {"seq": slot(y, 1 - x, c)}
    sibling = {"seq": slot(y, x, 1 - c)}
    z_plus = {"tp": xh * 4 + (z + 1) % 4}
    z_minus = {"tp": xh * 4 + (z + 3) % 4}
    x_far = {"tp": (1 - xh) * 4 + z}

    barrier = pltpu.get_barrier_semaphore()
    partners = (y_plus, y_minus, x_near, sibling, z_plus, z_minus, x_far)
    for partner in partners:
        pl.semaphore_signal(barrier, inc=1, device_id=partner, device_id_type=MESH)
    kv[s] = own_kv[...]
    og[t] = og_ref[...]
    pl.semaphore_wait(barrier, len(partners))

    def kv_copy(place, half, sem, device):
        part = kv.at[place, half]
        return remote(part, part, kv_send.at[sem], kv_recv.at[place, half], device)

    def kv_pair(place, sem, device):
        return [kv_copy(place, half, sem + half, device) for half in (0, 1)]

    near_place = slot(y, 1 - x, c)
    x_copies = kv_pair(s, 16, x_near)
    own_plus, own_minus = kv_pair(s, 18, y_plus), kv_pair(s, 20, y_minus)
    near_plus, near_minus = kv_pair(near_place, 22, y_plus), kv_pair(near_place, 24, y_minus)

    def ring_place(p, off):
        return slot((y + off) % 4, (x + p) % 2, c)

    def pass_plus(p):
        return kv_copy(ring_place(p, 3), 0, 26 + 2 * p, y_plus)

    def pass_minus(p):
        return kv_copy(ring_place(p, 1), 1, 27 + 2 * p, y_minus)

    def og_copy(place, half, sem, device):
        part = og.at[place, half]
        return remote(part, part, og_send.at[sem], og_recv.at[place, half], device)

    def og_pair(place, sem, device):
        return [og_copy(place, half, sem + half, device) for half in (0, 1)]

    far_place = (1 - xh) * 4 + z
    og_far = og_pair(t, 0, x_far)
    og_own_plus, og_own_minus = og_pair(t, 2, z_plus), og_pair(t, 4, z_minus)
    og_far_plus, og_far_minus = og_pair(far_place, 6, z_plus), og_pair(far_place, 8, z_minus)

    def og_place(a, off):
        return ((xh + a) % 2) * 4 + (z + off) % 4

    def og_pass_plus(a):
        return og_copy(og_place(a, 3), 0, 10 + 2 * a, z_plus)

    def og_pass_minus(a):
        return og_copy(og_place(a, 1), 1, 11 + 2 * a, z_minus)

    def og_wait(place):
        for half in (0, 1):
            og_copy(place, half, 0, z_plus).wait_recv()

    for copy in (
        x_copies[0], x_copies[1], own_plus[0], own_minus[1], own_plus[1], own_minus[0],
        *kv_pair(s, 0, sibling),
        og_far[0], og_far[1], og_own_plus[0], og_own_minus[1], og_own_plus[1], og_own_minus[0],
    ):
        copy.start()

    for h in range(HEADS_DEV):
        cols = slice(h * HEAD_SIZE, (h + 1) * HEAD_SIZE)
        scaled = q_ref[:, cols].astype(F32).T * LOG2_SCALE
        high = scaled.astype(BF16)
        qt[h, :HEAD_SIZE] = high
        qt[h, HEAD_SIZE:] = (scaled - high.astype(F32)).astype(BF16)

    def cols_of(h):
        return slice(h * HEAD_SIZE, (h + 1) * HEAD_SIZE)

    def scores_of(key, h, first):
        return dot(jnp.concatenate([key, key], axis=1), qt[h, :, first:])

    row_block = lax.broadcasted_iota(jnp.int32, (ROWS, ROWS), 0) // BLOCK
    col_block = lax.broadcasted_iota(jnp.int32, (ROWS, ROWS), 1) // BLOCK
    self_bias = jnp.where(row_block == col_block, 0.0, MASKED).astype(F32)
    bias[:, :ROWS] = self_bias

    for h in range(HEADS_DEV):
        scores = scores_of(noisy_kv[0, :, cols_of(h)], h, ROWS) + bias[:, :ROWS]
        top = jnp.max(scores, axis=0, keepdims=True)
        weights = jnp.exp2(scores - top)
        stat[0, h : h + 1, :ROWS] = jnp.full((1, ROWS), LOWEST, F32)
        stat[0, h : h + 1, ROWS:] = top
        stat[1, h : h + 1, :ROWS] = jnp.zeros((1, ROWS), F32)
        stat[1, h : h + 1, ROWS:] = jnp.sum(weights, axis=0, keepdims=True)
        acc[cols_of(h), :ROWS] = jnp.zeros((HEAD_SIZE, ROWS), F32)
        acc[cols_of(h), ROWS:] = dot_tn(noisy_kv[1, :, cols_of(h)], weights.astype(BF16))

    def set_bias(place):
        position = kv[place, 0, ROWS:, :HEAD_SIZE].astype(F32)
        offset = lax.broadcasted_iota(jnp.int32, (BLOCK, HEAD_SIZE), 0).astype(F32)
        for b in range(POS_ROWS):
            code = position[b : b + 1] * float(BLOCK) + offset
            for n in range(BOTH // HEAD_SIZE):
                lanes = slice(n * HEAD_SIZE, (n + 1) * HEAD_SIZE)
                bias[b * BLOCK : (b + 1) * BLOCK, lanes] = jnp.where(
                    code <= limit_ref[0:1, lanes], 0.0, MASKED
                ).astype(F32)

    def forward_step(i, carry):
        g, d, e = i // 4, (i % 4) // 2, i % 2
        mid = ((g + 1) % 4) // 2
        p = (1 - mid) * e + mid * (g - 1)
        off = mid * (3 - 2 * e) + (1 - mid) * 2 * (g // 3)
        place = slot((y + off) % 4, (x + p) % 2, (c + d) % 2)

        @pl.when(i == 8)
        def _():
            og_wait(og_place(0, 3))
            og_pass_plus(0).start()
            og_wait(og_place(0, 1))
            og_pass_minus(0).start()

        @pl.when(i == 12)
        def _():
            og_wait(far_place)
            for n in (0, 1):
                og_far_plus[n].start()
                og_far_minus[1 - n].start()

        @pl.when(i > 0)
        def _():
            for half in (0, 1):
                kv_copy(place, half, 0, sibling).wait_recv()

        @pl.when(i == 1)
        def _():
            for n in (0, 1):
                near_plus[n].start()
                near_minus[1 - n].start()

        for p_now, at in ((0, 4), (1, 8)):

            @pl.when(i == at)
            def _():
                pass_plus(p_now).start()

            @pl.when(i == at + 1)
            def _():
                pass_minus(p_now).start()

        @pl.when((i > 0) & (d == 0))
        def _():
            for copy in kv_pair(place, 2 * (2 * g + e), sibling):
                copy.start()

        set_bias(place)
        for h in range(HEADS_DEV):
            scores = scores_of(kv[place, 0, :ROWS, cols_of(h)], h, 0) + bias[...]
            old = stat[0, h : h + 1]
            top = jnp.maximum(old, jnp.max(scores, axis=0, keepdims=True))
            weights = jnp.exp2(scores - top)
            factor = jnp.exp2(old - top)
            stat[0, h : h + 1] = top
            stat[1, h : h + 1] = stat[1, h : h + 1] * factor + jnp.sum(
                weights, axis=0, keepdims=True
            )
            acc[cols_of(h)] = acc[cols_of(h)] * factor + dot_tn(
                kv[place, 1, :ROWS, cols_of(h)], weights.astype(BF16)
            )
        return carry

    lax.fori_loop(0, 16, forward_step, 0)

    for h in range(HEADS_DEV):
        total = stat[1, h : h + 1]
        out = acc[cols_of(h)] / total
        att_t[cols_of(h)] = out.astype(BF16)
        att[:, cols_of(h)] = out.T.astype(BF16)
        stat[0, h : h + 1] = stat[0, h : h + 1] + jnp.log2(total)

    def columns(j):
        return pl.ds(pl.multiple_of(j * WIDTH, HEAD_SIZE), WIDTH)

    def mix_step(j, carry):
        mixp[j] = dot(att[...], w_ref[:, columns(j)]).astype(BF16).reshape(2, ROWS, WIDTH)
        return carry

    lax.fori_loop(0, 8, mix_step, 0)

    half_rows = INNER_DEV // 2
    head_t[...] = jnp.zeros((INNER_DEV, BOTH), F32)

    def w_copy(j):
        return remote(w_out.at[j], w_recv.at[j], ws_send.at[j], ws_recv.at[j], sibling)

    def projection_step(k, carry):
        u = k // 6
        off = (1 - u) * ((3 * (k % 3)) % 5) + u * 2
        a = (1 - u) * (k // 3) + u * (k - 6)
        j = og_place(a, off)

        @pl.when(k >= 4)
        def _():
            og_wait(j)

        @pl.when(k == 4)
        def _():
            og_pass_plus(1).start()

        @pl.when(k == 5)
        def _():
            og_pass_minus(1).start()

        grads = og[j].reshape(BOTH, WIDTH)
        head_t[...] += dot_nt(w_ref[:, columns(j)], grads)
        theirs = att_t[pl.ds(pl.multiple_of((1 - c) * half_rows, 16), half_rows)]
        w_out[j] = dot(theirs, grads).astype(BF16).reshape(2, half_rows // 2, WIDTH)
        w_copy(j).start()
        mine = att_t[pl.ds(pl.multiple_of(c * half_rows, 16), half_rows)]
        w_pair[j] = dot(mine, grads).astype(BF16).reshape(2, half_rows // 2, WIDTH)
        return carry

    lax.fori_loop(0, 8, projection_step, 0)

    mix = RingReduce(
        lambda p, r: mixp.at[og_place(p, r)], m_via, m_ring, m_cross, m_send, m_rsem,
        z_plus, z_minus, x_far,
    )
    weight = RingReduce(
        lambda p, r: w_pair.at[((y + r) % 4) * 2 + (x + p) % 2], w_via, w_ring, w_cross,
        w_send, w_rsem, y_plus, y_minus, x_near,
    )
    turns = [(1, 2), (0, 2), (1, 1), (1, 3), (0, 1), (0, 3), (1, 0), (0, 0)]
    term = RingReduce(
        lambda p, r: t_recv.at[turns.index((p, r))], t_via, t_ring, t_cross,
        t_send, t_rsem, y_plus, y_minus, x_near,
    )

    for p in (1, 0):
        mix.start("far", p)
        mix.start("near", p)

    for h in range(HEADS_DEV):
        grad = head_t[cols_of(h)]
        rounded = grad.astype(BF16)
        head[:, cols_of(h)] = grad.T.astype(BF16)
        stat[1, h : h + 1] = jnp.sum(
            rounded.astype(F32) * att_t[cols_of(h)].astype(F32), axis=0, keepdims=True
        )
        att_t[cols_of(h)] = rounded
        dq[cols_of(h)] = jnp.zeros((HEAD_SIZE, BOTH), F32)
    head_tb = att_t

    def w_sum(j, carry):
        w_copy(j).wait_recv()
        w_pair[j] = (w_pair[j].astype(F32) + w_recv[j].astype(F32)).astype(BF16)
        return carry

    lax.fori_loop(0, 8, w_sum, 0)
    for p in (1, 0):
        weight.start("far", p)
        weight.start("near", p)

    def backward_tile(key, value, h, first, masks):
        scores = scores_of(key, h, first) + masks
        probs = jnp.exp2(scores - stat[0, h : h + 1, first:])
        value_term = dot(probs.astype(BF16), head[first:, cols_of(h)])
        prob_grad = dot(value, head_tb[cols_of(h), first:])
        score_grad = (probs * (prob_grad - stat[1, h : h + 1, first:])).astype(BF16)
        key_term = dot(score_grad, q_ref[first:, cols_of(h)]) * SCALE
        dq[cols_of(h), first:] += dot_tn(key, score_grad)
        return key_term.astype(BF16), value_term.astype(BF16)

    bias[:, :ROWS] = self_bias
    for h in range(HEADS_DEV):
        key_term, value_term = backward_tile(
            noisy_kv[0, :, cols_of(h)], noisy_kv[1, :, cols_of(h)], h, ROWS, bias[:, :ROWS]
        )
        kg_ref[1, :, cols_of(h)] = key_term
        vg_ref[1, :, cols_of(h)] = value_term

    def t_copy(j):
        return remote(t_out.at[j], t_recv.at[j], ts_send.at[j], ts_recv.at[j], sibling)

    def backward_step(i, carry):
        j, d = i // 2, 1 - i % 2
        g, e = j // 2, j % 2
        mid = ((g + 1) % 4) // 2
        off = mid * (1 + 2 * e) + (1 - mid) * 2 * (1 - g // 3)
        p = mid * (2 - g) + (1 - mid) * (1 - e)
        place = slot((y + off) % 4, (x + p) % 2, (c + d) % 2)

        @pl.when(i == 2)
        def _():
            weight.join(1)
            weight.join(0)

        @pl.when(i == 5)
        def _():
            mix.join(1)

        @pl.when(i == 9)
        def _():
            weight.to_partner()

        @pl.when(i == 10)
        def _():
            mix.join(0)

        @pl.when(i == 14)
        def _():
            term.to_partner()

        set_bias(place)
        for h in range(HEADS_DEV):
            key_term, value_term = backward_tile(
                kv[place, 0, :ROWS, cols_of(h)], kv[place, 1, :ROWS, cols_of(h)], h, 0, bias[...]
            )
            t_mine[0, :, cols_of(h)] = key_term
            t_mine[1, :, cols_of(h)] = value_term

        @pl.when(d == 1)
        def _():
            t_out[j] = t_mine[...]
            t_copy(j).start()

        @pl.when(d == 0)
        def _():
            t_copy(j).wait_recv()
            t_recv[j] = (t_recv[j].astype(F32) + t_mine[...].astype(F32)).astype(BF16)

        for n, (p_now, r) in enumerate(turns):
            if r == 0:
                continue

            @pl.when(i == 2 * n + 1)
            def _():
                if r == 2:
                    term.start("far", p_now)
                else:
                    which = (0,) if r == 1 else (1,)
                    term.start("near", p_now, which)
                    term.join(p_now, which)

        return carry

    lax.fori_loop(0, 16, backward_step, 0)

    for h in range(HEADS_DEV):
        qg_ref[:, cols_of(h)] = (dq[cols_of(h)] * SCALE).T.astype(BF16)

    mix.to_partner()

    w_final[...] = weight.result().reshape(half_rows, WIDTH)
    final_copy = remote(w_final, w_other, wf_sem.at[0], wf_sem.at[1], sibling)
    final_copy.start()

    terms = term.result().astype(BF16)
    kg_ref[0] = terms[0]
    vg_ref[0] = terms[1]

    final_copy.wait_recv()
    wg_ref[pl.ds(pl.multiple_of(c * half_rows, 16), half_rows)] = w_final[...]
    wg_ref[pl.ds(pl.multiple_of((1 - c) * half_rows, 16), half_rows)] = w_other[...]

    mixed_ref[...] = mix.result().astype(BF16)

    for copy in (*x_copies, *own_plus, *own_minus, *near_plus, *near_minus):
        copy.wait_send()
    for n in range(8):
        for copy in kv_pair(s, 2 * n, sibling):
            copy.wait_send()
        w_copy(n).wait_send()
        t_copy(n).wait_send()
    for p in (0, 1):
        pass_plus(p).wait_send()
        pass_minus(p).wait_send()
        og_pass_plus(p).wait_send()
        og_pass_minus(p).wait_send()
    for copy in (*og_far, *og_own_plus, *og_own_minus, *og_far_plus, *og_far_minus):
        copy.wait_send()
    mix.finish()
    weight.finish()
    term.finish()
    final_copy.wait_send()


def local(queries, keys, values, block_order, out_weight, out_grad):
    position = block_order.astype(F32)
    marks = jnp.broadcast_to(position.astype(BF16)[:, None], (POS_ROWS, INNER_DEV))
    own_kv = jnp.stack([jnp.concatenate([a[0], marks], axis=0) for a in (keys, values)])
    noisy_kv = jnp.stack([keys[1], values[1]])
    first = jnp.repeat(position * BLOCK, BLOCK)
    offsets = jnp.tile(jnp.arange(BLOCK, dtype=F32), POS_ROWS)
    limit = jnp.broadcast_to(jnp.concatenate([first + offsets, first - 1.0]), (8, BOTH))
    unit = (2, ROWS, INNER_DEV)
    w_unit = (2, INNER_DEV // 4, WIDTH)
    m_unit = (2, ROWS, WIDTH)

    def buffer(*shape, dtype=BF16):
        return pltpu.VMEM(shape, dtype)

    def sums(u):
        return [buffer(2, *u), buffer(2, 2, *u), buffer(*u)]

    scratch = [
        buffer(16, 2, ROWS + POS_ROWS, INNER_DEV),
        buffer(8, *m_unit),
        buffer(HEADS_DEV, 2 * HEAD_SIZE, BOTH),
        buffer(INNER_DEV, BOTH, dtype=F32),
        buffer(2, 8, BOTH, dtype=F32),
        buffer(INNER_DEV, BOTH),
        buffer(BOTH, INNER_DEV),
        buffer(ROWS, BOTH, dtype=F32),
        buffer(INNER_DEV, BOTH, dtype=F32),
        buffer(BOTH, INNER_DEV),
        buffer(INNER_DEV, BOTH, dtype=F32),
        buffer(8, *m_unit), *sums(m_unit),
        buffer(8, *w_unit), buffer(8, *w_unit), buffer(8, *w_unit), *sums(w_unit),
        buffer(INNER_DEV // 2, WIDTH, dtype=F32), buffer(INNER_DEV // 2, WIDTH, dtype=F32),
        buffer(8, *unit), buffer(8, *unit), buffer(*unit), *sums(unit),
        pltpu.SemaphoreType.DMA((30,)), pltpu.SemaphoreType.DMA((16, 2)),
        pltpu.SemaphoreType.DMA((14,)), pltpu.SemaphoreType.DMA((8, 2)),
        pltpu.SemaphoreType.DMA((13,)), pltpu.SemaphoreType.DMA((13,)),
        pltpu.SemaphoreType.DMA((13,)), pltpu.SemaphoreType.DMA((13,)),
        pltpu.SemaphoreType.DMA((8,)), pltpu.SemaphoreType.DMA((8,)),
        pltpu.SemaphoreType.DMA((2,)),
        pltpu.SemaphoreType.DMA((13,)), pltpu.SemaphoreType.DMA((13,)),
        pltpu.SemaphoreType.DMA((8,)), pltpu.SemaphoreType.DMA((8,)),
    ]
    whole = pl.BlockSpec(memory_space=pltpu.VMEM)
    mixed, query_grad, key_grad, value_grad, weight_grad = pl.pallas_call(
        layer_kernel,
        out_shape=(
            jax.ShapeDtypeStruct(m_unit, BF16),
            jax.ShapeDtypeStruct((BOTH, INNER_DEV), BF16),
            jax.ShapeDtypeStruct(unit, BF16),
            jax.ShapeDtypeStruct(unit, BF16),
            jax.ShapeDtypeStruct((INNER_DEV, WIDTH), F32),
        ),
        in_specs=[whole] * 6,
        out_specs=(whole,) * 5,
        scratch_shapes=scratch,
        compiler_params=pltpu.CompilerParams(
            collective_id=0, has_side_effects=True, vmem_limit_bytes=63 * 2**20
        ),
    )(queries.reshape(BOTH, INNER_DEV), own_kv, noisy_kv, out_weight, out_grad, limit)
    core = lax.axis_index("seq") % 2
    weight_grad = lax.dynamic_slice_in_dim(weight_grad, core * (WIDTH // 2), WIDTH // 2, axis=1)
    return (mixed, query_grad.reshape(unit), key_grad, value_grad, weight_grad)


def solution(mesh):
    return jax.shard_map(
        local,
        mesh=mesh,
        in_specs=(
            P(None, "seq", "tp"),
            P(None, "seq", "tp"),
            P(None, "seq", "tp"),
            P("seq"),
            P("tp", None),
            P(None, "seq", "tp"),
        ),
        out_specs=(
            P(None, "seq", "tp"),
            P(None, "seq", "tp"),
            P(None, "seq", "tp"),
            P(None, "seq", "tp"),
            P("tp", "seq"),
        ),
        check_vma=False,
    )
```

time: 557 us -> 142 us (0.25); the launches traced: 548 us -> 141 us
  waiting for transfers between devices: 185 us -> 0 us
  Pallas kernels: 0 us -> 128 us
  local copies, waits for them, and re-layouts: 101 us -> 9.79 us
  matrix products: 88.8 us -> 0 us
  starting transfers between devices: 73.5 us -> 0 us
  other arithmetic: 69.4 us -> 2.48 us
  between operations: 15.1 us -> 0.7 us
  blocking collectives: 11.5 us -> 0 us
    ppermute x92 -> x0, waiting for transfers between devices: 184 us -> none  [shifted(): return lax.ppermute(block, axis, route)]
    pallas_call x0 -> x1, Pallas kernels: none -> 128 us  [local(): pl.pallas_call(layer_kernel, out_shape=(jax.ShapeDtypeStruct(m_unit, BF16...]
    dot_general x121 -> x0, matrix products: 88.8 us -> none  [the longest x16 22.4 us: backward_tile(): jnp.einsum('qhd,khd->hqk', query_heads, key_heads, preferred_element_type...]
    ppermute x92 -> x0, starting transfers between devices: 73.2 us -> none  [shifted(): return lax.ppermute(block, axis, route)]
    convert_element_type x63 -> x1, other arithmetic: 53.4 us -> 0.66 us  [local(): position.astype(BF16)[:, None]]
    while x79 -> x0, local copies, waits for them, and re-layouts: 31.6 us -> none
    unnamed x67 -> x11, local copies, waits for them, and re-layouts: 35.2 us -> 6.27 us
    dynamic_slice x31 -> x1, local copies, waits for them, and re-layouts: 21.2 us -> 1.35 us  [local(): lax.dynamic_slice_in_dim(weight_grad, core * (WIDTH // 2), WIDTH // 2, ax...]
  transfers between devices with their start and end apart: 95 -> 0, of which waited for: 58 -> 0; matrix products, arithmetic and copies ran while one was open for 44% -> 0% of each run, Pallas kernels for 0% -> 0%
where the time goes in v1:
time: 142 us; the launch traced here: 141 us
  Pallas kernels  128 us (90%)
  local copies, waits for them, and re-layouts  9.79 us (7%)
  other arithmetic  2.48 us (2%)
    pallas_call x1, Pallas kernels, local(): pl.pallas_call(layer_kernel, out_shape=(jax.ShapeDtypeStruct(m_unit, BF16...  128 us
    unnamed x11, local copies, waits for them, and re-layouts  6.27 us

profile of v1, /device:TPU:1, one launch (start us, length us, event | category | flops | bytes accessed | tf_op | source)
XLA Modules:
  0.0 141.3 jit_solution(17110091899972763528)
XLA Ops:
  0.6 0.0 copy-start.2
  0.6 1.3 fusion
  2.0 0.7 convert_convert_fusion
  2.6 0.1 maximum_bitcast_fusion
  2.8 0.8 pad_maximum_fusion.own_kv
  3.6 0.8 pad_maximum_fusion.1.noisy_kv
  4.4 0.0 copy-done.2
  4.4 0.1 broadcast_in_dim.16
  4.4 0.1 sub.7
  4.5 0.1 iota_add_fusion
  4.6 0.1 add.17
  4.7 0.6 broadcast_in_dim.17.limit_ref
  5.3 128.3 %shard_map.101 = (bf16[2,256,640]{2,1,0:T(8,128)(2,1)}, bf16[512,384]{1,0:T(8,128)(2,1)}, bf16[2,256,384]{2,1,0:T(8,128)(2,1)}, bf16[2,256,384]{2,1,0:T(8,128)(2,1)}, f32[384,640]{1,0:T(8,128)}) custom-call(bf16[512,384]{1,0:T(8,128)(2,1)} %bitcast.10, bf16[2,272,384]{2,1,0:T(8,128)(2,1)} %pad_maximum_fusion.own_kv, ...), custom_call_target="tpu_custom_call" | custom-call | tf_op jit(solution)/shard_map/pallas_call | solution.py:556
  133.7 0.0 copy-start.1
  133.7 0.0 copy-start
  133.7 1.4 constant_dynamic-slice_fusion
  135.1 1.0 copy.11
  136.1 2.0 %copy.16 = bf16[2,256,640]{2,1,0:T(8,128)(2,1)} copy(bf16[2,256,640]{2,1,0:T(8,128)(2,1)} %get-tuple-element.35) | data formatting | bytes 1310720
  138.0 1.8 %copy.17 = bf16[2,256,384]{2,1,0:T(8,128)(2,1)} copy(bf16[2,256,384]{2,1,0:T(8,128)(2,1)} %bitcast.11) | data formatting | bytes 786432
  139.8 0.0 copy-done.1
  139.8 0.7 copy.18
  140.6 0.0 copy-done
  140.6 0.7 copy.19
  (3 shorter events, 0.0 us)
Async XLA Ops:
  0.6 3.7 %copy-start.2 = (s32[16]{0:T(128)S(1)}, s32[16]{0:T(128)}, u32[]{:S(2)}) copy-start(s32[16]{0:T(128)} %param.9) | copy-start | bytes 196
  133.7 6.2 %copy-start.1 = (bf16[2,256,384]{2,1,0:T(8,128)(2,1)S(1)}, bf16[2,256,384]{2,1,0:T(8,128)(2,1)}, u32[]{:S(2)}) copy-start(bf16[2,256,384]{2,1,0:T(8,128)(2,1)} %get-tuple-element.37) | copy-start | bytes 1179652
  133.7 6.9 %copy-start = (bf16[2,256,384]{2,1,0:T(8,128)(2,1)S(1)}, bf16[2,256,384]{2,1,0:T(8,128)(2,1)}, u32[]{:S(2)}) copy-start(bf16[2,256,384]{2,1,0:T(8,128)(2,1)} %get-tuple-element.38) | copy-start | bytes 1179652

commit v2 on v1

--- a/solution.py
+++ b/solution.py
@@ -48,6 +48,10 @@
     )
 
 
+def equal(a, n):
+    return (a + 16 - n) // 16 - (a + 15 - n) // 16
+
+
 class RingReduce:
     def __init__(self, piece, via, ring, cross, send, recv, plus, minus, partner):
         self.piece, self.via, self.ring, self.cross = piece, via, ring, cross
@@ -94,23 +98,24 @@
         self.copy("cross", 1, 0).wait_recv()
         return total + self.cross[...].astype(F32)
 
-    def finish(self):
-        for p in (0, 1):
+    def finish(self, sides=(0, 1)):
+        for p in sides:
             for kind in ("far", "near", "joint"):
                 for n in (0, 1):
                     self.copy(kind, p, n).wait_send()
-        self.copy("cross", 1, 0).wait_send()
+        if 1 in sides:
+            self.copy("cross", 1, 0).wait_send()
 
 
 def layer_kernel(
-    q_ref, own_kv, noisy_kv, w_ref, og_ref, limit_ref,
+    order_ref, q_ref, k_ref, v_ref, weight_ref, og_ref,
     mixed_ref, qg_ref, kg_ref, vg_ref, wg_ref,
-    kv, og, qt, acc, stat, att_t, att, bias, head_t, head, dq,
+    kv, noisy_kv, w_ref, og, limit, qt, acc, stat, att_t, att, bias, head_t, head, dq,
     mixp, m_via, m_ring, m_cross,
-    w_pair, w_out, w_recv, w_via, w_ring, w_cross, w_final, w_other,
+    w_pair, w_out, w_recv, w_x, w_via, w_ring, w_final, w_turn,
     t_out, t_recv, t_mine, t_via, t_ring, t_cross,
-    kv_send, kv_recv, og_send, og_recv,
-    m_send, m_rsem, w_send, w_rsem, ws_send, ws_recv, wf_sem,
+    load, kv_send, kv_recv, og_send, og_recv,
+    m_send, m_rsem, w_send, w_rsem, ws_send, ws_recv, wx_send, wx_recv, wf_sem,
     t_send, t_rsem, ts_send, ts_recv,
 ):
     s = lax.axis_index("seq")
@@ -133,24 +138,53 @@
     partners = (y_plus, y_minus, x_near, sibling, z_plus, z_minus, x_far)
     for partner in partners:
         pl.semaphore_signal(barrier, inc=1, device_id=partner, device_id_type=MESH)
-    kv[s] = own_kv[...]
-    og[t] = og_ref[...]
-    pl.semaphore_wait(barrier, len(partners))
+
+    loads = [
+        pltpu.make_async_copy(src, dst, load.at[n])
+        for n, (src, dst) in enumerate(
+            (
+                (k_ref.at[0], kv.at[s, 0, pl.ds(0, ROWS)]),
+                (v_ref.at[0], kv.at[s, 1, pl.ds(0, ROWS)]),
+                (og_ref, og.at[t]),
+                (k_ref.at[1], noisy_kv.at[0]),
+                (v_ref.at[1], noisy_kv.at[1]),
+                (weight_ref, w_ref),
+            )
+        )
+    ]
+    for copy in loads:
+        copy.start()
+
+    mark_row = lax.broadcasted_iota(jnp.int32, (POS_ROWS, INNER_DEV), 0)
+    lane = lax.broadcasted_iota(jnp.int32, (8, BOTH), 1)
+    lane_block = (lane % ROWS) // BLOCK
+    marks = jnp.zeros((POS_ROWS, INNER_DEV), F32)
+    start = jnp.zeros((8, BOTH), F32)
+    for b in range(POS_ROWS):
+        position = order_ref[b].astype(F32)
+        marks = jnp.where(mark_row == b, position, marks)
+        start = jnp.where(lane_block == b, position * float(BLOCK), start)
+    kv[s, 0, ROWS:] = marks.astype(BF16)
+    kv[s, 1, ROWS:] = marks.astype(BF16)
+    limit[...] = start + jnp.where(lane < ROWS, lane % BLOCK, -1).astype(F32)
 
     def kv_copy(place, half, sem, device):
         part = kv.at[place, half]
         return remote(part, part, kv_send.at[sem], kv_recv.at[place, half], device)
 
-    def kv_pair(place, sem, device):
-        return [kv_copy(place, half, sem + half, device) for half in (0, 1)]
-
     near_place = slot(y, 1 - x, c)
-    x_copies = kv_pair(s, 16, x_near)
-    own_plus, own_minus = kv_pair(s, 18, y_plus), kv_pair(s, 20, y_minus)
-    near_plus, near_minus = kv_pair(near_place, 22, y_plus), kv_pair(near_place, 24, y_minus)
 
     def ring_place(p, off):
         return slot((y + off) % 4, (x + p) % 2, c)
+
+    def own_copy(kind, half):
+        at = {"sibling": 0, "x": 16, "plus": 18, "minus": 20}[kind] + half
+        device = {"sibling": sibling, "x": x_near, "plus": y_plus, "minus": y_minus}[kind]
+        return kv_copy(s, half, at, device)
+
+    def near_copy(kind, half):
+        at = {"plus": 22, "minus": 24}[kind] + half
+        return kv_copy(near_place, half, at, {"plus": y_plus, "minus": y_minus}[kind])
 
     def pass_plus(p):
         return kv_copy(ring_place(p, 3), 0, 26 + 2 * p, y_plus)
@@ -162,13 +196,15 @@
         part = og.at[place, half]
         return remote(part, part, og_send.at[sem], og_recv.at[place, half], device)
 
-    def og_pair(place, sem, device):
-        return [og_copy(place, half, sem + half, device) for half in (0, 1)]
-
     far_place = (1 - xh) * 4 + z
-    og_far = og_pair(t, 0, x_far)
-    og_own_plus, og_own_minus = og_pair(t, 2, z_plus), og_pair(t, 4, z_minus)
-    og_far_plus, og_far_minus = og_pair(far_place, 6, z_plus), og_pair(far_place, 8, z_minus)
+
+    def og_own(kind, half):
+        at = {"far": 0, "plus": 2, "minus": 4}[kind] + half
+        return og_copy(t, half, at, {"far": x_far, "plus": z_plus, "minus": z_minus}[kind])
+
+    def og_far(kind, half):
+        at = {"plus": 6, "minus": 8}[kind] + half
+        return og_copy(far_place, half, at, {"plus": z_plus, "minus": z_minus}[kind])
 
     def og_place(a, off):
         return ((xh + a) % 2) * 4 + (z + off) % 4
@@ -179,16 +215,23 @@
     def og_pass_minus(a):
         return og_copy(og_place(a, 1), 1, 11 + 2 * a, z_minus)
 
-    def og_wait(place):
-        for half in (0, 1):
+    def og_wait(place, halves=(0, 1)):
+        for half in halves:
             og_copy(place, half, 0, z_plus).wait_recv()
 
-    for copy in (
-        x_copies[0], x_copies[1], own_plus[0], own_minus[1], own_plus[1], own_minus[0],
-        *kv_pair(s, 0, sibling),
-        og_far[0], og_far[1], og_own_plus[0], og_own_minus[1], og_own_plus[1], og_own_minus[0],
-    ):
-        copy.start()
+    loads[0].wait()
+    loads[1].wait()
+    loads[2].wait()
+    pl.semaphore_wait(barrier, len(partners))
+    for n in (0, 1):
+        own_copy("x", n).start()
+        own_copy("plus", n).start()
+        own_copy("minus", 1 - n).start()
+    for n in (0, 1):
+        og_own("plus", n).start()
+        og_own("minus", 1 - n).start()
+        og_own("far", n).start()
+        own_copy("sibling", n).start()
 
     for h in range(HEADS_DEV):
         cols = slice(h * HEAD_SIZE, (h + 1) * HEAD_SIZE)
@@ -203,6 +246,8 @@
     def scores_of(key, h, first):
         return dot(jnp.concatenate([key, key], axis=1), qt[h, :, first:])
 
+    loads[3].wait()
+    loads[4].wait()
     row_block = lax.broadcasted_iota(jnp.int32, (ROWS, ROWS), 0) // BLOCK
     col_block = lax.broadcasted_iota(jnp.int32, (ROWS, ROWS), 1) // BLOCK
     self_bias = jnp.where(row_block == col_block, 0.0, MASKED).astype(F32)
@@ -227,55 +272,55 @@
             for n in range(BOTH // HEAD_SIZE):
                 lanes = slice(n * HEAD_SIZE, (n + 1) * HEAD_SIZE)
                 bias[b * BLOCK : (b + 1) * BLOCK, lanes] = jnp.where(
-                    code <= limit_ref[0:1, lanes], 0.0, MASKED
+                    code <= limit[0:1, lanes], 0.0, MASKED
                 ).astype(F32)
 
     def forward_step(i, carry):
-        g, d, e = i // 4, (i % 4) // 2, i % 2
-        mid = ((g + 1) % 4) // 2
-        p = (1 - mid) * e + mid * (g - 1)
-        off = mid * (3 - 2 * e) + (1 - mid) * 2 * (g // 3)
+        n, d = i // 2, i % 2
+        p = n // 5 + (n + 6) // 7 - (n + 5) // 7
+        m = (n + 1) % 3
+        off = ((n + 6) // 8) * (m + 3 * ((2 - m) // 2))
         place = slot((y + off) % 4, (x + p) % 2, (c + d) % 2)
 
+        @pl.when(i == 6)
+        def _():
+            og_wait(og_place(0, 3), (0,))
+            og_pass_plus(0).start()
+            og_wait(og_place(0, 1), (1,))
+            og_pass_minus(0).start()
+
         @pl.when(i == 8)
         def _():
-            og_wait(og_place(0, 3))
-            og_pass_plus(0).start()
-            og_wait(og_place(0, 1))
-            og_pass_minus(0).start()
-
-        @pl.when(i == 12)
-        def _():
-            og_wait(far_place)
-            for n in (0, 1):
-                og_far_plus[n].start()
-                og_far_minus[1 - n].start()
-
-        @pl.when(i > 0)
-        def _():
-            for half in (0, 1):
+            og_wait(far_place, (0,))
+            og_far("plus", 0).start()
+
+        @pl.when(i == 10)
+        def _():
+            og_wait(far_place, (1,))
+            og_far("minus", 1).start()
+            og_far("plus", 1).start()
+            og_far("minus", 0).start()
+
+        for half in (0, 1):
+
+            @pl.when(i > 0)
+            def _():
                 kv_copy(place, half, 0, sibling).wait_recv()
 
-        @pl.when(i == 1)
-        def _():
-            for n in (0, 1):
-                near_plus[n].start()
-                near_minus[1 - n].start()
-
-        for p_now, at in ((0, 4), (1, 8)):
-
-            @pl.when(i == at)
+            @pl.when(i == 2)
             def _():
-                pass_plus(p_now).start()
-
-            @pl.when(i == at + 1)
+                near_copy("plus", half).start()
+                near_copy("minus", half).start()
+
+            for side, at in ((0, 4), (1, 10)):
+
+                @pl.when(i == at + 2 * half)
+                def _():
+                    (pass_minus if half else pass_plus)(side).start()
+
+            @pl.when((i > 0) & (d == 0))
             def _():
-                pass_minus(p_now).start()
-
-        @pl.when((i > 0) & (d == 0))
-        def _():
-            for copy in kv_pair(place, 2 * (2 * g + e), sibling):
-                copy.start()
+                kv_copy(place, half, 2 * n + half, sibling).start()
 
         set_bias(place)
         for h in range(HEADS_DEV):
@@ -294,6 +339,10 @@
         return carry
 
     lax.fori_loop(0, 16, forward_step, 0)
+    og_wait(og_place(1, 3), (0,))
+    og_pass_plus(1).start()
+    og_wait(og_place(1, 1), (1,))
+    og_pass_minus(1).start()
 
     for h in range(HEADS_DEV):
         total = stat[1, h : h + 1]
@@ -305,6 +354,8 @@
     def columns(j):
         return pl.ds(pl.multiple_of(j * WIDTH, HEAD_SIZE), WIDTH)
 
+    loads[5].wait()
+
     def mix_step(j, carry):
         mixp[j] = dot(att[...], w_ref[:, columns(j)]).astype(BF16).reshape(2, ROWS, WIDTH)
         return carry
@@ -317,52 +368,66 @@
     def w_copy(j):
         return remote(w_out.at[j], w_recv.at[j], ws_send.at[j], ws_recv.at[j], sibling)
 
+    def w_across(n):
+        return remote(w_pair.at[2 * n + 1 - x], w_x.at[n], wx_send.at[n], wx_recv.at[n], x_near)
+
+    def w_sum(j):
+        w_copy(j).wait_recv()
+        w_pair[j] = (w_pair[j].astype(F32) + w_recv[j].astype(F32)).astype(BF16)
+
+        @pl.when(j % 2 == 1 - x)
+        def _():
+            w_across(j // 2).start()
+
+    og_order = ((0, 0), (0, 3), (0, 1), (1, 0), (0, 2), (1, 3), (1, 1), (1, 2))
+
+    def og_at(k):
+        a = sum(u[0] * equal(k, n) for n, u in enumerate(og_order))
+        off = sum(u[1] * equal(k, n) for n, u in enumerate(og_order))
+        return og_place(a, off)
+
     def projection_step(k, carry):
-        u = k // 6
-        off = (1 - u) * ((3 * (k % 3)) % 5) + u * 2
-        a = (1 - u) * (k // 3) + u * (k - 6)
-        j = og_place(a, off)
-
-        @pl.when(k >= 4)
-        def _():
-            og_wait(j)
-
-        @pl.when(k == 4)
-        def _():
-            og_pass_plus(1).start()
-
-        @pl.when(k == 5)
-        def _():
-            og_pass_minus(1).start()
+        j = og_at(k)
+
+        for half, pieces in enumerate(((2, 4, 6, 7), (1, 4, 5, 7))):
+            for n in pieces:
+
+                @pl.when(k == n)
+                def _():
+                    og_wait(j, (half,))
 
         grads = og[j].reshape(BOTH, WIDTH)
-        head_t[...] += dot_nt(w_ref[:, columns(j)], grads)
         theirs = att_t[pl.ds(pl.multiple_of((1 - c) * half_rows, 16), half_rows)]
         w_out[j] = dot(theirs, grads).astype(BF16).reshape(2, half_rows // 2, WIDTH)
         w_copy(j).start()
         mine = att_t[pl.ds(pl.multiple_of(c * half_rows, 16), half_rows)]
         w_pair[j] = dot(mine, grads).astype(BF16).reshape(2, half_rows // 2, WIDTH)
+        head_t[...] += dot_nt(w_ref[:, columns(j)], grads)
+
+        @pl.when(k > 0)
+        def _():
+            w_sum(og_at(k - 1))
+
         return carry
-
-    lax.fori_loop(0, 8, projection_step, 0)
 
     mix = RingReduce(
         lambda p, r: mixp.at[og_place(p, r)], m_via, m_ring, m_cross, m_send, m_rsem,
         z_plus, z_minus, x_far,
     )
     weight = RingReduce(
-        lambda p, r: w_pair.at[((y + r) % 4) * 2 + (x + p) % 2], w_via, w_ring, w_cross,
+        lambda p, r: w_pair.at[((y + r) % 4) * 2 + (x + p) % 2], w_via, w_ring, None,
         w_send, w_rsem, y_plus, y_minus, x_near,
     )
-    turns = [(1, 2), (0, 2), (1, 1), (1, 3), (0, 1), (0, 3), (1, 0), (0, 0)]
+    mix.start("far", 1)
+    mix.start("near", 1)
+    lax.fori_loop(0, 8, projection_step, 0)
+    w_sum(og_at(7))
+
+    turns = [(1, 2), (1, 1), (1, 3), (1, 0), (0, 2), (0, 1), (0, 3), (0, 0)]
     term = RingReduce(
         lambda p, r: t_recv.at[turns.index((p, r))], t_via, t_ring, t_cross,
         t_send, t_rsem, y_plus, y_minus, x_near,
     )
-
-    for p in (1, 0):
-        mix.start("far", p)
-        mix.start("near", p)
 
     for h in range(HEADS_DEV):
         grad = head_t[cols_of(h)]
@@ -375,16 +440,6 @@
         dq[cols_of(h)] = jnp.zeros((HEAD_SIZE, BOTH), F32)
     head_tb = att_t
 
-    def w_sum(j, carry):
-        w_copy(j).wait_recv()
-        w_pair[j] = (w_pair[j].astype(F32) + w_recv[j].astype(F32)).astype(BF16)
-        return carry
-
-    lax.fori_loop(0, 8, w_sum, 0)
-    for p in (1, 0):
-        weight.start("far", p)
-        weight.start("near", p)
-
     def backward_tile(key, value, h, first, masks):
         scores = scores_of(key, h, first) + masks
         probs = jnp.exp2(scores - stat[0, h : h + 1, first:])
@@ -406,34 +461,49 @@
     def t_copy(j):
         return remote(t_out.at[j], t_recv.at[j], ts_send.at[j], ts_recv.at[j], sibling)
 
+    w_mine = pl.multiple_of(c * half_rows, 16)
+
+    def final_copy():
+        part = w_final.at[pl.ds(w_mine, half_rows)]
+        return remote(part, part, wf_sem.at[0], wf_sem.at[1], sibling)
+
     def backward_step(i, carry):
         j, d = i // 2, 1 - i % 2
-        g, e = j // 2, j % 2
-        mid = ((g + 1) % 4) // 2
-        off = mid * (1 + 2 * e) + (1 - mid) * 2 * (1 - g // 3)
-        p = mid * (2 - g) + (1 - mid) * (1 - e)
+        p, q = 1 - j // 4, j % 4
+        off = 2 * equal(q, 0) + equal(q, 1) + 3 * equal(q, 2)
         place = slot((y + off) % 4, (x + p) % 2, (c + d) % 2)
 
         @pl.when(i == 2)
         def _():
-            weight.join(1)
+            mix.join(1)
+            mix.start("far", 0)
+            mix.start("near", 0)
+
+        @pl.when(i == 6)
+        def _():
+            for n in range(4):
+                w_across(n).wait_recv()
+                mine = w_pair.at[2 * n + x]
+                mine[...] = (mine[...].astype(F32) + w_x[n].astype(F32)).astype(BF16)
+            weight.start("far", 0)
+            weight.start("near", 0)
+
+        @pl.when(i == 10)
+        def _():
             weight.join(0)
 
-        @pl.when(i == 5)
-        def _():
-            mix.join(1)
-
-        @pl.when(i == 9)
-        def _():
-            weight.to_partner()
-
-        @pl.when(i == 10)
-        def _():
-            mix.join(0)
+        @pl.when(i == 11)
+        def _():
+            term.to_partner()
+
+        @pl.when(i == 12)
+        def _():
+            mix.to_partner()
 
         @pl.when(i == 14)
         def _():
-            term.to_partner()
+            w_final[pl.ds(w_mine, half_rows)] = weight.gathered(0).reshape(half_rows, WIDTH)
+            final_copy().start()
 
         set_bias(place)
         for h in range(HEADS_DEV):
@@ -470,53 +540,62 @@
 
     lax.fori_loop(0, 16, backward_step, 0)
 
+    mix.join(0)
     for h in range(HEADS_DEV):
         qg_ref[:, cols_of(h)] = (dq[cols_of(h)] * SCALE).T.astype(BF16)
 
-    mix.to_partner()
-
-    w_final[...] = weight.result().reshape(half_rows, WIDTH)
-    final_copy = remote(w_final, w_other, wf_sem.at[0], wf_sem.at[1], sibling)
-    final_copy.start()
+
+    w_theirs = pl.multiple_of((1 - c) * half_rows, 16)
+    part = w_final.at[pl.ds(w_theirs, half_rows)]
+    remote(part, part, wf_sem.at[0], wf_sem.at[1], sibling).wait_recv()
+    for n in range(INNER_DEV // HEAD_SIZE):
+        w_turn[:, cols_of(n)] = w_final[cols_of(n)].T
+    wg_ref[...] = w_turn[pl.ds(pl.multiple_of(c * (WIDTH // 2), 8), WIDTH // 2)]
 
     terms = term.result().astype(BF16)
     kg_ref[0] = terms[0]
     vg_ref[0] = terms[1]
 
-    final_copy.wait_recv()
-    wg_ref[pl.ds(pl.multiple_of(c * half_rows, 16), half_rows)] = w_final[...]
-    wg_ref[pl.ds(pl.multiple_of((1 - c) * half_rows, 16), half_rows)] = w_other[...]
-
     mixed_ref[...] = mix.result().astype(BF16)
 
-    for copy in (*x_copies, *own_plus, *own_minus, *near_plus, *near_minus):
-        copy.wait_send()
+    for half in (0, 1):
+        for kind in ("x", "plus", "minus"):
+            own_copy(kind, half).wait_send()
+        for kind in ("plus", "minus"):
+            near_copy(kind, half).wait_send()
+            og_own(kind, half).wait_send()
+            og_far(kind, half).wait_send()
+        og_own("far", half).wait_send()
+        for n in range(8):
+            kv_copy(s, half, 2 * n + half, sibling).wait_send()
     for n in range(8):
-        for copy in kv_pair(s, 2 * n, sibling):
-            copy.wait_send()
         w_copy(n).wait_send()
         t_copy(n).wait_send()
+    for n in range(4):
+        w_across(n).wait_send()
     for p in (0, 1):
         pass_plus(p).wait_send()
         pass_minus(p).wait_send()
         og_pass_plus(p).wait_send()
         og_pass_minus(p).wait_send()
-    for copy in (*og_far, *og_own_plus, *og_own_minus, *og_far_plus, *og_far_minus):
-        copy.wait_send()
     mix.finish()
-    weight.finish()
+    weight.finish((0,))
     term.finish()
-    final_copy.wait_send()
+    final_copy().wait_send()
+
+
+def results_kernel(*refs):
+    count = len(refs) // 2
+    copies = [
+        pltpu.make_async_copy(refs[n], refs[count + n], refs[-1].at[n]) for n in range(count)
+    ]
+    for copy in copies:
+        copy.start()
+    for copy in copies:
+        copy.wait()
 
 
 def local(queries, keys, values, block_order, out_weight, out_grad):
-    position = block_order.astype(F32)
-    marks = jnp.broadcast_to(position.astype(BF16)[:, None], (POS_ROWS, INNER_DEV))
-    own_kv = jnp.stack([jnp.concatenate([a[0], marks], axis=0) for a in (keys, values)])
-    noisy_kv = jnp.stack([keys[1], values[1]])
-    first = jnp.repeat(position * BLOCK, BLOCK)
-    offsets = jnp.tile(jnp.arange(BLOCK, dtype=F32), POS_ROWS)
-    limit = jnp.broadcast_to(jnp.concatenate([first + offsets, first - 1.0]), (8, BOTH))
     unit = (2, ROWS, INNER_DEV)
     w_unit = (2, INNER_DEV // 4, WIDTH)
     m_unit = (2, ROWS, WIDTH)
@@ -529,7 +608,10 @@
 
     scratch = [
         buffer(16, 2, ROWS + POS_ROWS, INNER_DEV),
+        buffer(*unit),
+        buffer(*out_weight.shape),
         buffer(8, *m_unit),
+        buffer(8, BOTH, dtype=F32),
         buffer(HEADS_DEV, 2 * HEAD_SIZE, BOTH),
         buffer(INNER_DEV, BOTH, dtype=F32),
         buffer(2, 8, BOTH, dtype=F32),
@@ -540,38 +622,45 @@
         buffer(BOTH, INNER_DEV),
         buffer(INNER_DEV, BOTH, dtype=F32),
         buffer(8, *m_unit), *sums(m_unit),
-        buffer(8, *w_unit), buffer(8, *w_unit), buffer(8, *w_unit), *sums(w_unit),
-        buffer(INNER_DEV // 2, WIDTH, dtype=F32), buffer(INNER_DEV // 2, WIDTH, dtype=F32),
+        buffer(8, *w_unit), buffer(8, *w_unit), buffer(8, *w_unit), buffer(4, *w_unit),
+        *sums(w_unit)[:2], buffer(INNER_DEV, WIDTH, dtype=F32),
+        buffer(WIDTH, INNER_DEV, dtype=F32),
         buffer(8, *unit), buffer(8, *unit), buffer(*unit), *sums(unit),
-        pltpu.SemaphoreType.DMA((30,)), pltpu.SemaphoreType.DMA((16, 2)),
-        pltpu.SemaphoreType.DMA((14,)), pltpu.SemaphoreType.DMA((8, 2)),
-        pltpu.SemaphoreType.DMA((13,)), pltpu.SemaphoreType.DMA((13,)),
-        pltpu.SemaphoreType.DMA((13,)), pltpu.SemaphoreType.DMA((13,)),
-        pltpu.SemaphoreType.DMA((8,)), pltpu.SemaphoreType.DMA((8,)),
-        pltpu.SemaphoreType.DMA((2,)),
-        pltpu.SemaphoreType.DMA((13,)), pltpu.SemaphoreType.DMA((13,)),
-        pltpu.SemaphoreType.DMA((8,)), pltpu.SemaphoreType.DMA((8,)),
+        *(
+            pltpu.SemaphoreType.DMA(shape)
+            for shape in (
+                (6,), (30,), (16, 2), (14,), (8, 2), (13,), (13,), (13,), (13,),
+                (8,), (8,), (4,), (4,), (2,), (13,), (13,), (8,), (8,),
+            )
+        ),
     ]
     whole = pl.BlockSpec(memory_space=pltpu.VMEM)
-    mixed, query_grad, key_grad, value_grad, weight_grad = pl.pallas_call(
+    anywhere = pl.BlockSpec(memory_space=pl.ANY)
+    shapes = (
+        jax.ShapeDtypeStruct(m_unit, BF16),
+        jax.ShapeDtypeStruct((BOTH, INNER_DEV), BF16),
+        jax.ShapeDtypeStruct(unit, BF16),
+        jax.ShapeDtypeStruct(unit, BF16),
+        jax.ShapeDtypeStruct((WIDTH // 2, INNER_DEV), F32),
+    )
+    results = pl.pallas_call(
         layer_kernel,
-        out_shape=(
-            jax.ShapeDtypeStruct(m_unit, BF16),
-            jax.ShapeDtypeStruct((BOTH, INNER_DEV), BF16),
-            jax.ShapeDtypeStruct(unit, BF16),
-            jax.ShapeDtypeStruct(unit, BF16),
-            jax.ShapeDtypeStruct((INNER_DEV, WIDTH), F32),
-        ),
-        in_specs=[whole] * 6,
+        out_shape=shapes,
+        in_specs=[pl.BlockSpec(memory_space=pltpu.SMEM), whole] + [anywhere] * 4,
         out_specs=(whole,) * 5,
         scratch_shapes=scratch,
         compiler_params=pltpu.CompilerParams(
             collective_id=0, has_side_effects=True, vmem_limit_bytes=63 * 2**20
         ),
-    )(queries.reshape(BOTH, INNER_DEV), own_kv, noisy_kv, out_weight, out_grad, limit)
-    core = lax.axis_index("seq") % 2
-    weight_grad = lax.dynamic_slice_in_dim(weight_grad, core * (WIDTH // 2), WIDTH // 2, axis=1)
-    return (mixed, query_grad.reshape(unit), key_grad, value_grad, weight_grad)
+    )(block_order, queries.reshape(BOTH, INNER_DEV), keys, values, out_weight, out_grad)
+    mixed, query_grad, key_grad, value_grad, weight_grad = pl.pallas_call(
+        results_kernel,
+        out_shape=shapes,
+        in_specs=[whole] * 5,
+        out_specs=(anywhere,) * 5,
+        scratch_shapes=[pltpu.SemaphoreType.DMA((5,))],
+    )(*results)
+    return (mixed, query_grad.reshape(unit), key_grad, value_grad, weight_grad.T)
 
 
 def solution(mesh):

time: 142 us -> 123 us (0.87); the launches traced: 141 us -> 121 us
  local copies, waits for them, and re-layouts: 9.79 us -> 0 us
  Pallas kernels: 128 us -> 120 us
  other arithmetic: 2.48 us -> 0 us
    pallas_call x1 -> x2, Pallas kernels: 128 us -> 120 us  [the longest x1 117 us: local(): pl.pallas_call(layer_kernel, out_shape=shapes, in_specs=[pl.BlockSpec(mem...]
    unnamed x11 -> x0, local copies, waits for them, and re-layouts: 6.27 us -> none
    another operation x3 -> x0, other arithmetic: 1.73 us -> none  [the longest x2 0.94 us: local(): jnp.stack([jnp.concatenate([a[0], marks], axis=0) for a in (keys, values)])]
where the time goes in v2:
time: 123 us; the launch traced here: 121 us
  Pallas kernels  120 us (98%)
    pallas_call x1, Pallas kernels, local(): pl.pallas_call(layer_kernel, out_shape=shapes, in_specs=[pl.BlockSpec(mem...  117 us
    pallas_call x1, Pallas kernels, local(): pl.pallas_call(results_kernel, out_shape=shapes, in_specs=[whole] * 5, ou...  3.01 us

profile of v2, /device:TPU:1, one launch (start us, length us, event | category | flops | bytes accessed | tf_op | source)
XLA Modules:
  0.0 120.5 jit_solution(11719840111664526773)
XLA Ops:
  0.6 116.9 %shard_map.101 = (bf16[2,256,640]{2,1,0:T(8,128)(2,1)}, bf16[512,384]{1,0:T(8,128)(2,1)}, bf16[2,256,384]{2,1,0:T(8,128)(2,1)}, bf16[2,256,384]{2,1,0:T(8,128)(2,1)}, f32[320,384]{1,0:T(8,128)}) custom-call(s32[16]{0:T(128)} %order_ref.1, bf16[512,384]{1,0:T(8,128)(2,1)} %bitcast.3, bf16[2,256,384]{2,1,0:T(8,128)(2,1)} %k_ref.1, bf16[2,256,384]{2,1,0:T(8,128)(2,1)} %v_ref.1, ...), custom_call_target="tpu_custom_call" | custom-call | tf_op jit(solution)/shard_map/pallas_call | solution.py:646
  117.5 3.0 %shard_map.102 = (bf16[2,256,640]{2,1,0:T(8,128)(2,1)}, bf16[512,384]{1,0:T(8,128)(2,1)}, bf16[2,256,384]{2,1,0:T(8,128)(2,1)}, bf16[2,256,384]{2,1,0:T(8,128)(2,1)}, f32[320,384]{1,0:T(8,128)}) custom-call(bf16[2,256,640]{2,1,0:T(8,128)(2,1)} %get-tuple-element.15.refs_0_, bf16[512,384]{1,0:T(8,128)(2,1)} %get-tuple-element.16.refs_1_, ...), custom_call_target="tpu_custom_call" | custom-call | tf_op jit(solution)/shard_map/pallas_call | solution.py:656

commit v3 on v2

--- a/solution.py
+++ b/solution.py
@@ -15,6 +15,7 @@
 BOTH = 2 * ROWS
 POS_ROWS = ROWS // BLOCK
 INNER_DEV = HEADS_DEV * HEAD_SIZE
+SPLIT = 192
 WIDTH = 640
 MESH = pl.DeviceIdType.MESH
 F32 = jnp.float32
@@ -165,11 +166,10 @@
         marks = jnp.where(mark_row == b, position, marks)
         start = jnp.where(lane_block == b, position * float(BLOCK), start)
     kv[s, 0, ROWS:] = marks.astype(BF16)
-    kv[s, 1, ROWS:] = marks.astype(BF16)
     limit[...] = start + jnp.where(lane < ROWS, lane % BLOCK, -1).astype(F32)
 
     def kv_copy(place, half, sem, device):
-        part = kv.at[place, half]
+        part = kv.at[place, half, pl.ds(0, ROWS if half else ROWS + POS_ROWS)]
         return remote(part, part, kv_send.at[sem], kv_recv.at[place, half], device)
 
     near_place = slot(y, 1 - x, c)
@@ -192,32 +192,39 @@
     def pass_minus(p):
         return kv_copy(ring_place(p, 1), 1, 27 + 2 * p, y_minus)
 
-    def og_copy(place, half, sem, device):
-        part = og.at[place, half]
-        return remote(part, part, og_send.at[sem], og_recv.at[place, half], device)
+    def og_copy(place, half, sem, device, part=None):
+        rows = {None: pl.ds(0, ROWS), 0: pl.ds(0, SPLIT), 1: pl.ds(SPLIT, ROWS - SPLIT)}[part]
+        piece = og.at[place, half, rows]
+        recv = og_recv.at[place, half + (2 if part == 1 else 0)]
+        return remote(piece, piece, og_send.at[sem], recv, device)
 
     far_place = (1 - xh) * 4 + z
 
     def og_own(kind, half):
-        at = {"far": 0, "plus": 2, "minus": 4}[kind] + half
-        return og_copy(t, half, at, {"far": x_far, "plus": z_plus, "minus": z_minus}[kind])
+        if kind == "far":
+            return og_copy(t, half, half, x_far, 0)
+        at = {"plus": 2, "minus": 4}[kind] + half
+        return og_copy(t, half, at, {"plus": z_plus, "minus": z_minus}[kind])
 
     def og_far(kind, half):
         at = {"plus": 6, "minus": 8}[kind] + half
-        return og_copy(far_place, half, at, {"plus": z_plus, "minus": z_minus}[kind])
+        return og_copy(far_place, half, at, {"plus": z_plus, "minus": z_minus}[kind], 0)
 
     def og_place(a, off):
         return ((xh + a) % 2) * 4 + (z + off) % 4
 
     def og_pass_plus(a):
-        return og_copy(og_place(a, 3), 0, 10 + 2 * a, z_plus)
+        return og_copy(og_place(a, 3), 0, 10 + 2 * a, z_plus, 0 if a else None)
 
     def og_pass_minus(a):
-        return og_copy(og_place(a, 1), 1, 11 + 2 * a, z_minus)
-
-    def og_wait(place, halves=(0, 1)):
+        return og_copy(og_place(a, 1), 1, 11 + 2 * a, z_minus, 0 if a else None)
+
+    def og_late(off, half):
+        return og_copy(og_place(0, off), half, 14 + 2 * off + half, x_far, 1)
+
+    def og_wait(place, halves=(0, 1), part=None):
         for half in halves:
-            og_copy(place, half, 0, z_plus).wait_recv()
+            og_copy(place, half, 0, z_plus, part).wait_recv()
 
     loads[0].wait()
     loads[1].wait()
@@ -232,6 +239,8 @@
         og_own("minus", 1 - n).start()
         og_own("far", n).start()
         own_copy("sibling", n).start()
+    for n in (0, 1):
+        og_late(0, n).start()
 
     for h in range(HEADS_DEV):
         cols = slice(h * HEAD_SIZE, (h + 1) * HEAD_SIZE)
@@ -275,6 +284,26 @@
                     code <= limit[0:1, lanes], 0.0, MASKED
                 ).astype(F32)
 
+    def columns(j):
+        return pl.ds(pl.multiple_of(j * WIDTH, HEAD_SIZE), WIDTH)
+
+    half_rows = INNER_DEV // 2
+    head_t[...] = jnp.zeros((INNER_DEV, BOTH), F32)
+
+    loads[5].wait()
+
+    og_order = ((0, 0), (0, 3), (0, 1), (1, 0), (0, 2), (1, 3), (1, 1), (1, 2))
+
+    def og_at(k):
+        a = sum(u[0] * equal(k, n) for n, u in enumerate(og_order))
+        off = sum(u[1] * equal(k, n) for n, u in enumerate(og_order))
+        return og_place(a, off)
+
+    def head_step(k, carry):
+        j = og_at(k)
+        head_t[...] += dot_nt(w_ref[:, columns(j)], og[j].reshape(BOTH, WIDTH))
+        return carry
+
     def forward_step(i, carry):
         n, d = i // 2, i % 2
         p = n // 5 + (n + 6) // 7 - (n + 5) // 7
@@ -291,15 +320,31 @@
 
         @pl.when(i == 8)
         def _():
-            og_wait(far_place, (0,))
+            og_wait(far_place, (0,), 0)
             og_far("plus", 0).start()
+            og_wait(og_place(0, 3), (1,))
+            og_wait(og_place(0, 1), (0,))
+            for off in (3, 1):
+                for half in (0, 1):
+                    og_late(off, half).start()
+
+        @pl.when(i == 12)
+        def _():
+            og_wait(og_place(0, 2))
+            for half in (0, 1):
+                og_late(2, half).start()
 
         @pl.when(i == 10)
         def _():
-            og_wait(far_place, (1,))
+            og_wait(far_place, (1,), 0)
             og_far("minus", 1).start()
             og_far("plus", 1).start()
             og_far("minus", 0).start()
+
+        @pl.when(i == 14)
+        def _():
+            og_wait(far_place, (0, 1), 1)
+            lax.fori_loop(0, 5, head_step, 0)
 
         for half in (0, 1):
 
@@ -339,9 +384,9 @@
         return carry
 
     lax.fori_loop(0, 16, forward_step, 0)
-    og_wait(og_place(1, 3), (0,))
+    og_wait(og_place(1, 3), (0,), 0)
     og_pass_plus(1).start()
-    og_wait(og_place(1, 1), (1,))
+    og_wait(og_place(1, 1), (1,), 0)
     og_pass_minus(1).start()
 
     for h in range(HEADS_DEV):
@@ -351,19 +396,10 @@
         att[:, cols_of(h)] = out.T.astype(BF16)
         stat[0, h : h + 1] = stat[0, h : h + 1] + jnp.log2(total)
 
-    def columns(j):
-        return pl.ds(pl.multiple_of(j * WIDTH, HEAD_SIZE), WIDTH)
-
-    loads[5].wait()
-
-    def mix_step(j, carry):
+    def mix_step(side, n, carry):
+        j = side * 4 + n
         mixp[j] = dot(att[...], w_ref[:, columns(j)]).astype(BF16).reshape(2, ROWS, WIDTH)
         return carry
-
-    lax.fori_loop(0, 8, mix_step, 0)
-
-    half_rows = INNER_DEV // 2
-    head_t[...] = jnp.zeros((INNER_DEV, BOTH), F32)
 
     def w_copy(j):
         return remote(w_out.at[j], w_recv.at[j], ws_send.at[j], ws_recv.at[j], sibling)
@@ -379,22 +415,20 @@
         def _():
             w_across(j // 2).start()
 
-    og_order = ((0, 0), (0, 3), (0, 1), (1, 0), (0, 2), (1, 3), (1, 1), (1, 2))
-
-    def og_at(k):
-        a = sum(u[0] * equal(k, n) for n, u in enumerate(og_order))
-        off = sum(u[1] * equal(k, n) for n, u in enumerate(og_order))
-        return og_place(a, off)
-
     def projection_step(k, carry):
         j = og_at(k)
 
-        for half, pieces in enumerate(((2, 4, 6, 7), (1, 4, 5, 7))):
+        for half, pieces in enumerate(((6, 7), (5, 7))):
             for n in pieces:
 
                 @pl.when(k == n)
                 def _():
-                    og_wait(j, (half,))
+                    og_wait(j, (half,), 0)
+
+        @pl.when(k > 4)
+        def _():
+            og_wait(j, (0, 1), 1)
+            head_step(k, 0)
 
         grads = og[j].reshape(BOTH, WIDTH)
         theirs = att_t[pl.ds(pl.multiple_of((1 - c) * half_rows, 16), half_rows)]
@@ -402,7 +436,6 @@
         w_copy(j).start()
         mine = att_t[pl.ds(pl.multiple_of(c * half_rows, 16), half_rows)]
         w_pair[j] = dot(mine, grads).astype(BF16).reshape(2, half_rows // 2, WIDTH)
-        head_t[...] += dot_nt(w_ref[:, columns(j)], grads)
 
         @pl.when(k > 0)
         def _():
@@ -418,12 +451,16 @@
         lambda p, r: w_pair.at[((y + r) % 4) * 2 + (x + p) % 2], w_via, w_ring, None,
         w_send, w_rsem, y_plus, y_minus, x_near,
     )
+    lax.fori_loop(0, 5, projection_step, 0)
+    lax.fori_loop(0, 4, functools.partial(mix_step, 1 - xh), 0)
     mix.start("far", 1)
     mix.start("near", 1)
-    lax.fori_loop(0, 8, projection_step, 0)
+    lax.fori_loop(5, 7, projection_step, 0)
+    lax.fori_loop(0, 4, functools.partial(mix_step, xh), 0)
+    lax.fori_loop(7, 8, projection_step, 0)
     w_sum(og_at(7))
 
-    turns = [(1, 2), (1, 1), (1, 3), (1, 0), (0, 2), (0, 1), (0, 3), (0, 0)]
+    turns = [(1, 2), (0, 2), (1, 1), (1, 3), (0, 1), (0, 3), (1, 0), (0, 0)]
     term = RingReduce(
         lambda p, r: t_recv.at[turns.index((p, r))], t_via, t_ring, t_cross,
         t_send, t_rsem, y_plus, y_minus, x_near,
@@ -450,6 +487,84 @@
         dq[cols_of(h), first:] += dot_tn(key, score_grad)
         return key_term.astype(BF16), value_term.astype(BF16)
 
+    def t_copy(j):
+        return remote(t_out.at[j], t_recv.at[j], ts_send.at[j], ts_recv.at[j], sibling)
+
+    w_mine = pl.multiple_of(c * half_rows, 16)
+
+    def final_copy():
+        part = w_final.at[pl.ds(w_mine, half_rows)]
+        return remote(part, part, wf_sem.at[0], wf_sem.at[1], sibling)
+
+    def backward_step(i, carry):
+        odd, last, second = i % 2, equal(i, 15), equal(i, 1)
+        late = (i + 13) // 16
+        d = 1 - ((1 - odd) * late + last + second)
+        j = late * (odd * ((i + 1) // 2) + (1 - odd) * (i // 2 - 1) - last) + equal(i, 2)
+        p = sum(turn[0] * equal(j, n) for n, turn in enumerate(turns))
+        off = sum(turn[1] * equal(j, n) for n, turn in enumerate(turns))
+        place = slot((y + off) % 4, (x + p) % 2, (c + d) % 2)
+
+        @pl.when(i == 2)
+        def _():
+            mix.join(1)
+            mix.start("far", 0)
+            mix.start("near", 0)
+
+        @pl.when(i == 13)
+        def _():
+            for n in range(4):
+                w_across(n).wait_recv()
+                mine = w_pair.at[2 * n + x]
+                mine[...] = (mine[...].astype(F32) + w_x[n].astype(F32)).astype(BF16)
+            weight.start("far", 0)
+            weight.start("near", 0)
+
+        @pl.when(i == 15)
+        def _():
+            term.to_partner()
+
+        @pl.when(i == 11)
+        def _():
+            mix.to_partner()
+
+        set_bias(place)
+        for h in range(HEADS_DEV):
+            key_term, value_term = backward_tile(
+                kv[place, 0, :ROWS, cols_of(h)], kv[place, 1, :ROWS, cols_of(h)], h, 0, bias[...]
+            )
+            t_mine[0, :, cols_of(h)] = key_term
+            t_mine[1, :, cols_of(h)] = value_term
+
+        @pl.when(d == 1)
+        def _():
+            t_out[j] = t_mine[...]
+            t_copy(j).start()
+
+        @pl.when(d == 0)
+        def _():
+            t_copy(j).wait_recv()
+            t_recv[j] = (t_recv[j].astype(F32) + t_mine[...].astype(F32)).astype(BF16)
+
+        for n, (p_now, r) in enumerate(turns):
+            if r == 0:
+                continue
+
+            @pl.when(i == (2 * n + 2 if n else 1))
+            def _():
+                if r == 2:
+                    term.start("far", p_now)
+                else:
+                    which = (0,) if r == 1 else (1,)
+                    term.start("near", p_now, which)
+                    term.join(p_now, which)
+
+        return carry
+
+    lax.fori_loop(0, 16, backward_step, 0)
+
+    mix.join(0)
+    weight.join(0)
     bias[:, :ROWS] = self_bias
     for h in range(HEADS_DEV):
         key_term, value_term = backward_tile(
@@ -458,92 +573,17 @@
         kg_ref[1, :, cols_of(h)] = key_term
         vg_ref[1, :, cols_of(h)] = value_term
 
-    def t_copy(j):
-        return remote(t_out.at[j], t_recv.at[j], ts_send.at[j], ts_recv.at[j], sibling)
-
-    w_mine = pl.multiple_of(c * half_rows, 16)
-
-    def final_copy():
-        part = w_final.at[pl.ds(w_mine, half_rows)]
-        return remote(part, part, wf_sem.at[0], wf_sem.at[1], sibling)
-
-    def backward_step(i, carry):
-        j, d = i // 2, 1 - i % 2
-        p, q = 1 - j // 4, j % 4
-        off = 2 * equal(q, 0) + equal(q, 1) + 3 * equal(q, 2)
-        place = slot((y + off) % 4, (x + p) % 2, (c + d) % 2)
-
-        @pl.when(i == 2)
-        def _():
-            mix.join(1)
-            mix.start("far", 0)
-            mix.start("near", 0)
-
-        @pl.when(i == 6)
-        def _():
-            for n in range(4):
-                w_across(n).wait_recv()
-                mine = w_pair.at[2 * n + x]
-                mine[...] = (mine[...].astype(F32) + w_x[n].astype(F32)).astype(BF16)
-            weight.start("far", 0)
-            weight.start("near", 0)
-
-        @pl.when(i == 10)
-        def _():
-            weight.join(0)
-
-        @pl.when(i == 11)
-        def _():
-            term.to_partner()
-
-        @pl.when(i == 12)
-        def _():
-            mix.to_partner()
-
-        @pl.when(i == 14)
-        def _():
-            w_final[pl.ds(w_mine, half_rows)] = weight.gathered(0).reshape(half_rows, WIDTH)
-            final_copy().start()
-
-        set_bias(place)
-        for h in range(HEADS_DEV):
-            key_term, value_term = backward_tile(
-                kv[place, 0, :ROWS, cols_of(h)], kv[place, 1, :ROWS, cols_of(h)], h, 0, bias[...]
-            )
-            t_mine[0, :, cols_of(h)] = key_term
-            t_mine[1, :, cols_of(h)] = value_term
-
-        @pl.when(d == 1)
-        def _():
-            t_out[j] = t_mine[...]
-            t_copy(j).start()
-
-        @pl.when(d == 0)
-        def _():
-            t_copy(j).wait_recv()
-            t_recv[j] = (t_recv[j].astype(F32) + t_mine[...].astype(F32)).astype(BF16)
-
-        for n, (p_now, r) in enumerate(turns):
-            if r == 0:
-                continue
-
-            @pl.when(i == 2 * n + 1)
-            def _():
-                if r == 2:
-                    term.start("far", p_now)
-                else:
-                    which = (0,) if r == 1 else (1,)
-                    term.start("near", p_now, which)
-                    term.join(p_now, which)
-
-        return carry
-
-    lax.fori_loop(0, 16, backward_step, 0)
-
-    mix.join(0)
     for h in range(HEADS_DEV):
         qg_ref[:, cols_of(h)] = (dq[cols_of(h)] * SCALE).T.astype(BF16)
 
+
+    terms = term.result().astype(BF16)
+    kg_ref[0] = terms[0]
+    vg_ref[0] = terms[1]
+
+    w_final[pl.ds(w_mine, half_rows)] = weight.gathered(0).reshape(half_rows, WIDTH)
+    final_copy().start()
+    mixed_ref[...] = mix.result().astype(BF16)
 
     w_theirs = pl.multiple_of((1 - c) * half_rows, 16)
     part = w_final.at[pl.ds(w_theirs, half_rows)]
@@ -551,12 +591,6 @@
     for n in range(INNER_DEV // HEAD_SIZE):
         w_turn[:, cols_of(n)] = w_final[cols_of(n)].T
     wg_ref[...] = w_turn[pl.ds(pl.multiple_of(c * (WIDTH // 2), 8), WIDTH // 2)]
-
-    terms = term.result().astype(BF16)
-    kg_ref[0] = terms[0]
-    vg_ref[0] = terms[1]
-
-    mixed_ref[...] = mix.result().astype(BF16)
 
     for half in (0, 1):
         for kind in ("x", "plus", "minus"):
@@ -565,6 +599,8 @@
             near_copy(kind, half).wait_send()
             og_own(kind, half).wait_send()
             og_far(kind, half).wait_send()
+        for off in range(4):
+            og_late(off, half).wait_send()
         og_own("far", half).wait_send()
         for n in range(8):
             kv_copy(s, half, 2 * n + half, sibling).wait_send()
@@ -629,7 +665,7 @@
         *(
             pltpu.SemaphoreType.DMA(shape)
             for shape in (
-                (6,), (30,), (16, 2), (14,), (8, 2), (13,), (13,), (13,), (13,),
+                (6,), (30,), (16, 2), (22,), (8, 4), (13,), (13,), (13,), (13,),
                 (8,), (8,), (4,), (4,), (2,), (13,), (13,), (8,), (8,),
             )
         ),

time: 123 us -> 114 us (0.927); the launches traced: 121 us -> 114 us
  Pallas kernels: 120 us -> 113 us
    pallas_call x1, Pallas kernels: 117 us -> 110 us  [local(): pl.pallas_call(layer_kernel, out_shape=shapes, in_specs=[pl.BlockSpec(mem...]
where the time goes in v3:
time: 114 us
  Pallas kernels  113 us (99%)
    pallas_call x1, Pallas kernels, local(): pl.pallas_call(layer_kernel, out_shape=shapes, in_specs=[pl.BlockSpec(mem...  110 us
    pallas_call x1, Pallas kernels, local(): pl.pallas_call(results_kernel, out_shape=shapes, in_specs=[whole] * 5, ou...  3.01 us

profile of v3, /device:TPU:1, one launch (start us, length us, event | category | flops | bytes accessed | tf_op | source)
XLA Modules:
  0.0 114.0 jit_solution(14671869684405929188)
XLA Ops:
  0.6 110.4 %shard_map.101 = (bf16[2,256,640]{2,1,0:T(8,128)(2,1)}, bf16[512,384]{1,0:T(8,128)(2,1)}, bf16[2,256,384]{2,1,0:T(8,128)(2,1)}, bf16[2,256,384]{2,1,0:T(8,128)(2,1)}, f32[320,384]{1,0:T(8,128)}) custom-call(s32[16]{0:T(128)} %order_ref.1, bf16[512,384]{1,0:T(8,128)(2,1)} %bitcast.3, bf16[2,256,384]{2,1,0:T(8,128)(2,1)} %k_ref.1, bf16[2,256,384]{2,1,0:T(8,128)(2,1)} %v_ref.1, ...), custom_call_target="tpu_custom_call" | custom-call | tf_op jit(solution)/shard_map/pallas_call | solution.py:682
  111.0 3.0 %shard_map.102 = (bf16[2,256,640]{2,1,0:T(8,128)(2,1)}, bf16[512,384]{1,0:T(8,128)(2,1)}, bf16[2,256,384]{2,1,0:T(8,128)(2,1)}, bf16[2,256,384]{2,1,0:T(8,128)(2,1)}, f32[320,384]{1,0:T(8,128)}) custom-call(bf16[2,256,640]{2,1,0:T(8,128)(2,1)} %get-tuple-element.15.refs_0_, bf16[512,384]{1,0:T(8,128)(2,1)} %get-tuple-element.16.refs_1_, ...), custom_call_target="tpu_custom_call" | custom-call | tf_op jit(solution)/shard_map/pallas_call | solution.py:692

commit v4 on v3

--- a/solution.py
+++ b/solution.py
@@ -109,9 +109,9 @@
 
 
 def layer_kernel(
-    order_ref, q_ref, k_ref, v_ref, weight_ref, og_ref,
+    order_ref, q_in, k_ref, v_ref, weight_ref, og_ref,
     mixed_ref, qg_ref, kg_ref, vg_ref, wg_ref,
-    kv, noisy_kv, w_ref, og, limit, qt, acc, stat, att_t, att, bias, head_t, head, dq,
+    kv, noisy_kv, w_ref, q_ref, og, limit, qt, acc, stat, att_t, att, bias, head_t, head, dq,
     mixp, m_via, m_ring, m_cross,
     w_pair, w_out, w_recv, w_x, w_via, w_ring, w_final, w_turn,
     t_out, t_recv, t_mine, t_via, t_ring, t_cross,
@@ -150,10 +150,11 @@
                 (k_ref.at[1], noisy_kv.at[0]),
                 (v_ref.at[1], noisy_kv.at[1]),
                 (weight_ref, w_ref),
+                (q_in, q_ref),
             )
         )
     ]
-    for copy in loads:
+    for copy in loads[:3]:
         copy.start()
 
     mark_row = lax.broadcasted_iota(jnp.int32, (POS_ROWS, INNER_DEV), 0)
@@ -241,6 +242,9 @@
         own_copy("sibling", n).start()
     for n in (0, 1):
         og_late(0, n).start()
+    for n in (6, 3, 4, 5):
+        loads[n].start()
+    loads[6].wait()
 
     for h in range(HEADS_DEV):
         cols = slice(h * HEAD_SIZE, (h + 1) * HEAD_SIZE)
@@ -443,9 +447,16 @@
 
         return carry
 
-    mix = RingReduce(
-        lambda p, r: mixp.at[og_place(p, r)], m_via, m_ring, m_cross, m_send, m_rsem,
-        z_plus, z_minus, x_far,
+    half_stream = ROWS // 2
+    mix_a, mix_b = (
+        RingReduce(
+            lambda p, r, first=n * half_stream: mixp.at[
+                og_place(p, r), :, pl.ds(first, half_stream)
+            ],
+            m_via.at[n], m_ring.at[n], m_cross.at[n], m_send.at[n], m_rsem.at[n],
+            z_plus, z_minus, x_far,
+        )
+        for n in (0, 1)
     )
     weight = RingReduce(
         lambda p, r: w_pair.at[((y + r) % 4) * 2 + (x + p) % 2], w_via, w_ring, None,
@@ -453,14 +464,15 @@
     )
     lax.fori_loop(0, 5, projection_step, 0)
     lax.fori_loop(0, 4, functools.partial(mix_step, 1 - xh), 0)
-    mix.start("far", 1)
-    mix.start("near", 1)
+    mix_a.start("far", 1)
+    mix_a.start("near", 1)
+    mix_b.start("far", 1)
     lax.fori_loop(5, 7, projection_step, 0)
     lax.fori_loop(0, 4, functools.partial(mix_step, xh), 0)
     lax.fori_loop(7, 8, projection_step, 0)
     w_sum(og_at(7))
 
-    turns = [(1, 2), (0, 2), (1, 1), (1, 3), (0, 1), (0, 3), (1, 0), (0, 0)]
+    turns = [(1, 2), (0, 2), (1, 1), (1, 3), (1, 0), (0, 1), (0, 3), (0, 0)]
     term = RingReduce(
         lambda p, r: t_recv.at[turns.index((p, r))], t_via, t_ring, t_cross,
         t_send, t_rsem, y_plus, y_minus, x_near,
@@ -505,13 +517,24 @@
         off = sum(turn[1] * equal(j, n) for n, turn in enumerate(turns))
         place = slot((y + off) % 4, (x + p) % 2, (c + d) % 2)
 
-        @pl.when(i == 2)
-        def _():
-            mix.join(1)
-            mix.start("far", 0)
-            mix.start("near", 0)
-
-        @pl.when(i == 13)
+        @pl.when(i == 1)
+        def _():
+            mix_a.join(1)
+            mix_b.start("near", 1)
+
+        @pl.when(i == 6)
+        def _():
+            mix_b.join(1)
+            for part in (mix_a, mix_b):
+                part.start("far", 0)
+            for part in (mix_a, mix_b):
+                part.start("near", 0)
+
+        @pl.when(i == 8)
+        def _():
+            mix_a.to_partner()
+
+        @pl.when(i == 9)
         def _():
             for n in range(4):
                 w_across(n).wait_recv()
@@ -520,13 +543,15 @@
             weight.start("far", 0)
             weight.start("near", 0)
 
+        @pl.when(i == 12)
+        def _():
+            mix_b.to_partner()
+
         @pl.when(i == 15)
         def _():
+            weight.join(0)
+            term.join(0)
             term.to_partner()
-
-        @pl.when(i == 11)
-        def _():
-            mix.to_partner()
 
         set_bias(place)
         for h in range(HEADS_DEV):
@@ -557,14 +582,15 @@
                 else:
                     which = (0,) if r == 1 else (1,)
                     term.start("near", p_now, which)
-                    term.join(p_now, which)
+                    if p_now == 1:
+                        term.join(p_now, which)
 
         return carry
 
     lax.fori_loop(0, 16, backward_step, 0)
 
-    mix.join(0)
-    weight.join(0)
+    mix_a.join(0)
+    mix_b.join(0)
     bias[:, :ROWS] = self_bias
     for h in range(HEADS_DEV):
         key_term, value_term = backward_tile(
@@ -577,20 +603,20 @@
         qg_ref[:, cols_of(h)] = (dq[cols_of(h)] * SCALE).T.astype(BF16)
 
 
-    terms = term.result().astype(BF16)
-    kg_ref[0] = terms[0]
-    vg_ref[0] = terms[1]
-
     w_final[pl.ds(w_mine, half_rows)] = weight.gathered(0).reshape(half_rows, WIDTH)
     final_copy().start()
-    mixed_ref[...] = mix.result().astype(BF16)
-
     w_theirs = pl.multiple_of((1 - c) * half_rows, 16)
     part = w_final.at[pl.ds(w_theirs, half_rows)]
     remote(part, part, wf_sem.at[0], wf_sem.at[1], sibling).wait_recv()
     for n in range(INNER_DEV // HEAD_SIZE):
         w_turn[:, cols_of(n)] = w_final[cols_of(n)].T
     wg_ref[...] = w_turn[pl.ds(pl.multiple_of(c * (WIDTH // 2), 8), WIDTH // 2)]
+
+    terms = term.result().astype(BF16)
+    kg_ref[0] = terms[0]
+    vg_ref[0] = terms[1]
+    mixed_ref[:, :half_stream] = mix_a.result().astype(BF16)
+    mixed_ref[:, half_stream:] = mix_b.result().astype(BF16)
 
     for half in (0, 1):
         for kind in ("x", "plus", "minus"):
@@ -614,7 +640,8 @@
         pass_minus(p).wait_send()
         og_pass_plus(p).wait_send()
         og_pass_minus(p).wait_send()
-    mix.finish()
+    mix_a.finish()
+    mix_b.finish()
     weight.finish((0,))
     term.finish()
     final_copy().wait_send()
@@ -639,13 +666,14 @@
     def buffer(*shape, dtype=BF16):
         return pltpu.VMEM(shape, dtype)
 
-    def sums(u):
-        return [buffer(2, *u), buffer(2, 2, *u), buffer(*u)]
+    def sums(u, *parts):
+        return [buffer(*parts, 2, *u), buffer(*parts, 2, 2, *u), buffer(*parts, *u)]
 
     scratch = [
         buffer(16, 2, ROWS + POS_ROWS, INNER_DEV),
         buffer(*unit),
         buffer(*out_weight.shape),
+        buffer(BOTH, INNER_DEV),
         buffer(8, *m_unit),
         buffer(8, BOTH, dtype=F32),
         buffer(HEADS_DEV, 2 * HEAD_SIZE, BOTH),
@@ -657,7 +685,7 @@
         buffer(INNER_DEV, BOTH, dtype=F32),
         buffer(BOTH, INNER_DEV),
         buffer(INNER_DEV, BOTH, dtype=F32),
-        buffer(8, *m_unit), *sums(m_unit),
+        buffer(8, *m_unit), *sums((2, ROWS // 2, WIDTH), 2),
         buffer(8, *w_unit), buffer(8, *w_unit), buffer(8, *w_unit), buffer(4, *w_unit),
         *sums(w_unit)[:2], buffer(INNER_DEV, WIDTH, dtype=F32),
         buffer(WIDTH, INNER_DEV, dtype=F32),
@@ -665,7 +693,7 @@
         *(
             pltpu.SemaphoreType.DMA(shape)
             for shape in (
-                (6,), (30,), (16, 2), (22,), (8, 4), (13,), (13,), (13,), (13,),
+                (7,), (30,), (16, 2), (22,), (8, 4), (2, 13), (2, 13), (13,), (13,),
                 (8,), (8,), (4,), (4,), (2,), (13,), (13,), (8,), (8,),
             )
         ),
@@ -682,7 +710,7 @@
     results = pl.pallas_call(
         layer_kernel,
         out_shape=shapes,
-        in_specs=[pl.BlockSpec(memory_space=pltpu.SMEM), whole] + [anywhere] * 4,
+        in_specs=[pl.BlockSpec(memory_space=pltpu.SMEM)] + [anywhere] * 5,
         out_specs=(whole,) * 5,
         scratch_shapes=scratch,
         compiler_params=pltpu.CompilerParams(

time: 114 us -> 111 us (0.974)
  Pallas kernels: 113 us -> 110 us
    pallas_call x1, Pallas kernels: 110 us -> 107 us  [local(): pl.pallas_call(layer_kernel, out_shape=shapes, in_specs=[pl.BlockSpec(mem...]
where the time goes in v4:
time: 111 us
  Pallas kernels  110 us (99%)
    pallas_call x1, Pallas kernels, local(): pl.pallas_call(layer_kernel, out_shape=shapes, in_specs=[pl.BlockSpec(mem...  107 us
    pallas_call x1, Pallas kernels, local(): pl.pallas_call(results_kernel, out_shape=shapes, in_specs=[whole] * 5, ou...  3.01 us

profile of v4, /device:TPU:1, one launch (start us, length us, event | category | flops | bytes accessed | tf_op | source)
XLA Modules:
  0.0 110.6 jit_solution(15974452182713287170)
XLA Ops:
  0.6 107.0 %shard_map.101 = (bf16[2,256,640]{2,1,0:T(8,128)(2,1)}, bf16[512,384]{1,0:T(8,128)(2,1)}, bf16[2,256,384]{2,1,0:T(8,128)(2,1)}, bf16[2,256,384]{2,1,0:T(8,128)(2,1)}, f32[320,384]{1,0:T(8,128)}) custom-call(s32[16]{0:T(128)} %order_ref.1, bf16[512,384]{1,0:T(8,128)(2,1)} %bitcast.3, bf16[2,256,384]{2,1,0:T(8,128)(2,1)} %k_ref.1, bf16[2,256,384]{2,1,0:T(8,128)(2,1)} %v_ref.1, ...), custom_call_target="tpu_custom_call" | custom-call | tf_op jit(solution)/shard_map/pallas_call | solution.py:710
  107.6 3.0 %shard_map.102 = (bf16[2,256,640]{2,1,0:T(8,128)(2,1)}, bf16[512,384]{1,0:T(8,128)(2,1)}, bf16[2,256,384]{2,1,0:T(8,128)(2,1)}, bf16[2,256,384]{2,1,0:T(8,128)(2,1)}, f32[320,384]{1,0:T(8,128)}) custom-call(bf16[2,256,640]{2,1,0:T(8,128)(2,1)} %get-tuple-element.15.refs_0_, bf16[512,384]{1,0:T(8,128)(2,1)} %get-tuple-element.16.refs_1_, ...), custom_call_target="tpu_custom_call" | custom-call | tf_op jit(solution)/shard_map/pallas_call | solution.py:720

commit v5 on v4

--- a/solution.py
+++ b/solution.py
@@ -709,12 +709,12 @@
     )
     results = pl.pallas_call(
         layer_kernel,
-        out_shape=shapes,
+        out_shape=tuple(pltpu.VMEM(a.shape, a.dtype) for a in shapes),
         in_specs=[pl.BlockSpec(memory_space=pltpu.SMEM)] + [anywhere] * 5,
         out_specs=(whole,) * 5,
         scratch_shapes=scratch,
         compiler_params=pltpu.CompilerParams(
-            collective_id=0, has_side_effects=True, vmem_limit_bytes=63 * 2**20
+            collective_id=0, has_side_effects=True, vmem_limit_bytes=60 * 2**20
         ),
     )(block_order, queries.reshape(BOTH, INNER_DEV), keys, values, out_weight, out_grad)
     mixed, query_grad, key_grad, value_grad, weight_grad = pl.pallas_call(
@@ -723,7 +723,7 @@
         in_specs=[whole] * 5,
         out_specs=(anywhere,) * 5,
         scratch_shapes=[pltpu.SemaphoreType.DMA((5,))],
-    )(*results)
+    )(*(pltpu.with_memory_space_constraint(a, pltpu.VMEM) for a in results))
     return (mixed, query_grad.reshape(unit), key_grad, value_grad, weight_grad.T)
 
 

time: 111 us -> 108 us (0.973)
  Pallas kernels: 110 us -> 107 us
    pallas_call x1, Pallas kernels: 3.01 us -> 1.43 us  [local(): pl.pallas_call(results_kernel, out_shape=shapes, in_specs=[whole] * 5, ou...]
    pallas_call x1, Pallas kernels: 107 us -> 106 us  [local(): pl.pallas_call(layer_kernel, out_shape=tuple((pltpu.VMEM(a.shape, a.dtype...]
where the time goes in v5:
time: 108 us
  Pallas kernels  107 us (99%)
    pallas_call x1, Pallas kernels, local(): pl.pallas_call(layer_kernel, out_shape=tuple((pltpu.VMEM(a.shape, a.dtype...  106 us

profile of v5, /device:TPU:1, one launch (start us, length us, event | category | flops | bytes accessed | tf_op | source)
XLA Modules:
  0.0 107.6 jit_solution(14912963761904863991)
XLA Ops:
  0.6 105.6 %shard_map.101 = (bf16[2,256,640]{2,1,0:T(8,128)(2,1)S(1)}, bf16[512,384]{1,0:T(8,128)(2,1)S(1)}, bf16[2,256,384]{2,1,0:T(8,128)(2,1)S(1)}, bf16[2,256,384]{2,1,0:T(8,128)(2,1)S(1)}, f32[320,384]{1,0:T(8,128)S(1)}) custom-call(s32[16]{0:T(128)} %order_ref.1, bf16[512,384]{1,0:T(8,128)(2,1)} %bitcast.3, bf16[2,256,384]{2,1,0:T(8,128)(2,1)} %k_ref.1, ...), custom_call_target="tpu_custom_call" | custom-call | tf_op jit(solution)/shard_map/pallas_call | solution.py:710
  106.2 1.4 %shard_map.102 = (bf16[2,256,640]{2,1,0:T(8,128)(2,1)}, bf16[512,384]{1,0:T(8,128)(2,1)}, bf16[2,256,384]{2,1,0:T(8,128)(2,1)}, bf16[2,256,384]{2,1,0:T(8,128)(2,1)}, f32[320,384]{1,0:T(8,128)}) custom-call(bf16[2,256,640]{2,1,0:T(8,128)(2,1)S(1)} %get-tuple-element.15.refs_0_, bf16[512,384]{1,0:T(8,128)(2,1)S(1)} %get-tuple-element.16.refs_1_, ...), custom_call_target="tpu_custom_call" | custom-call | tf_op jit(solution)/shard_map/pallas_call | solution.py:720

commit v6 on v5

--- a/solution.py
+++ b/solution.py
@@ -229,12 +229,12 @@
 
     loads[0].wait()
     loads[1].wait()
-    loads[2].wait()
     pl.semaphore_wait(barrier, len(partners))
     for n in (0, 1):
         own_copy("x", n).start()
         own_copy("plus", n).start()
         own_copy("minus", 1 - n).start()
+    loads[2].wait()
     for n in (0, 1):
         og_own("plus", n).start()
         og_own("minus", 1 - n).start()

time: 108 us -> 108 us (level)
  no operation moved by 1% of the time
where the time goes in v6:
time: 108 us
  Pallas kernels  107 us (99%)
    pallas_call x1, Pallas kernels, local(): pl.pallas_call(layer_kernel, out_shape=tuple((pltpu.VMEM(a.shape, a.dtype...  106 us

profile of v6, /device:TPU:1, one launch (start us, length us, event | category | flops | bytes accessed | tf_op | source)
XLA Modules:
  0.0 107.6 jit_solution(7613809027463045151)
XLA Ops:
  0.6 105.6 %shard_map.101 = (bf16[2,256,640]{2,1,0:T(8,128)(2,1)S(1)}, bf16[512,384]{1,0:T(8,128)(2,1)S(1)}, bf16[2,256,384]{2,1,0:T(8,128)(2,1)S(1)}, bf16[2,256,384]{2,1,0:T(8,128)(2,1)S(1)}, f32[320,384]{1,0:T(8,128)S(1)}) custom-call(s32[16]{0:T(128)} %order_ref.1, bf16[512,384]{1,0:T(8,128)(2,1)} %bitcast.3, bf16[2,256,384]{2,1,0:T(8,128)(2,1)} %k_ref.1, ...), custom_call_target="tpu_custom_call" | custom-call | tf_op jit(solution)/shard_map/pallas_call | solution.py:710
  106.2 1.4 %shard_map.102 = (bf16[2,256,640]{2,1,0:T(8,128)(2,1)}, bf16[512,384]{1,0:T(8,128)(2,1)}, bf16[2,256,384]{2,1,0:T(8,128)(2,1)}, bf16[2,256,384]{2,1,0:T(8,128)(2,1)}, f32[320,384]{1,0:T(8,128)}) custom-call(bf16[2,256,640]{2,1,0:T(8,128)(2,1)S(1)} %get-tuple-element.15.refs_0_, bf16[512,384]{1,0:T(8,128)(2,1)S(1)} %get-tuple-element.16.refs_1_, ...), custom_call_target="tpu_custom_call" | custom-call | tf_op jit(solution)/shard_map/pallas_call | solution.py:720
